TPU v7x, 32 devices: a whole 2x2x4 slice. The times are simulated.
32 devices in a mesh: dp: 8 (over z, x), seq: 4 (over y, core).
Axes of the slice: x: 2, y: 2, z: 4, core: 2. Of those that a mesh axis runs over, the one named last changes fastest.
Arguments:
- hidden_in: bfloat16 [8, 1024, 768], P('dp', 'seq'), may hold values from -6 to 6
- condition: bfloat16 [8, 256], P('dp'), may hold values from -6 to 6
- qkv_weight: bfloat16 [768, 2304], P('dp'), may hold values from -0.21875 to 0.21875
- out_weight: bfloat16 [768, 768], P('dp'), may hold values from -3.5 to 3.5
- gate_up_weight: bfloat16 [768, 6144], P('dp'), may hold values from -0.21875 to 0.21875
- down_weight: bfloat16 [3072, 768], P('dp'), may hold values from -0.109375 to 0.109375
- ada_weight: bfloat16 [256, 4608], P('dp'), may hold values from -0.375 to 0.375
- pair_embed: bfloat16 [66, 256], replicated, may hold values from -6 to 6
- pair_gain: bfloat16 [256], replicated, may hold values from 0.099609375 to 1.8984375
- pair_weight: bfloat16 [256, 12], replicated, may hold values from -0.375 to 0.375
- valid_len: int32 [8], P('dp'), may hold values from 512 to 1024, as said below
- chain_break: int32 [8], P('dp'), may hold values from 256 to 1535
- out_grad: bfloat16 [8, 1024, 768], P('dp', 'seq'), may hold values from -6 to 6
Outputs:
- result: bfloat16 [8, 1024, 768], P('dp', 'seq')
- input_grad: bfloat16 [8, 1024, 768], P('dp', 'seq')
- grad_qkv: float32 [768, 2304], P('dp')
- grad_out: float32 [768, 768], P('dp')
- grad_gate_up: float32 [768, 6144], P('dp')
- grad_down: float32 [3072, 768], P('dp')
- grad_ada: float32 [256, 4608], P('dp')
- grad_embed: float32 [66, 256], replicated
- grad_gain: float32 [256], replicated
- grad_pair: float32 [256, 12], replicated
Inputs may be any that keep to these rules, and one draw needn't show every extreme that they name: Positions from valid_len on are padding keys; in each aligned group of 1 items one item has live residues in the last residue block of the seq axis; the first item has all 1024 residues. Positions from chain_break on form a second chain; a value of 1024 or more means one chain.
All inputs are finite; a program needn't handle non-finite values.
Results may differ from a plain program's by a relative error of at most 0.023.
Values may be sent and summed in bfloat16 or wider, within the bound.
A program may use at most 192 MiB of HBM per device.

v0:
```python
import jax
import jax.numpy as jnp
from jax import lax
from jax.sharding import PartitionSpec as P

H = 12
DH = 64
RR = 32
CLASSES = 66


HIGHEST = lax.Precision.HIGHEST


def layer_norm(values):
    average = jnp.mean(values, axis=-1, keepdims=True)
    centered = values - average
    inv_std = lax.rsqrt(jnp.mean(centered * centered, axis=-1, keepdims=True) + 1e-06)
    return (centered * inv_std, inv_std)


def norm_back(upstream, normal, inv_std):
    return inv_std * (
        upstream
        - jnp.mean(upstream, axis=-1, keepdims=True)
        - normal * jnp.mean(upstream * normal, axis=-1, keepdims=True)
    )


def pair_table(pair_embed, pair_gain, pair_weight):
    average = jnp.mean(pair_embed, axis=-1, keepdims=True)
    centered = pair_embed - average
    normal = centered * lax.rsqrt(jnp.mean(centered * centered, axis=-1, keepdims=True) + 1e-05)
    return jnp.dot(normal * pair_gain, pair_weight, precision=HIGHEST)


def pair_classes(query_pos, key_pos, breaks):
    query_side = query_pos[None, :, None] >= breaks[:, None, None]
    key_side = key_pos[None, None, :] >= breaks[:, None, None]
    offset = jnp.clip(query_pos[:, None] - key_pos[None, :], -RR, RR) + RR
    return jnp.where(query_side == key_side, offset[None], 2 * RR + 1)


def score_block(queries4, key_block, table, query_pos, key_pos, breaks, lengths):
    items, width = (key_block.shape[0], key_block.shape[1])
    keys4 = key_block.reshape(items, width, H, DH)
    raw = jnp.einsum("irhd,inhd->ihrn", queries4, keys4, preferred_element_type=jnp.float32) * 0.125
    classes = pair_classes(query_pos, key_pos, breaks)
    bias = jnp.moveaxis(jnp.take(table, classes, axis=0), -1, 1)
    alive = (key_pos[None, :] < lengths[:, None])[:, None, None, :]
    return (jnp.where(alive, raw + bias, -1e30), alive, classes)


def body(
    hidden_in,
    condition,
    qkv_weight,
    out_weight,
    gate_up_weight,
    down_weight,
    ada_weight,
    pair_embed,
    pair_gain,
    pair_weight,
    valid_len,
    chain_break,
    out_grad,
):
    items, rows, width = hidden_in.shape
    seq_count = lax.axis_size("seq")
    full_qkv, full_out, full_gate_up, full_down, full_ada = (
        lax.all_gather(qkv_weight, "dp", axis=0, tiled=True),
        lax.all_gather(out_weight, "dp", axis=0, tiled=True),
        lax.all_gather(gate_up_weight, "dp", axis=0, tiled=True),
        lax.all_gather(down_weight, "dp", axis=0, tiled=True),
        lax.all_gather(ada_weight, "dp", axis=0, tiled=True),
    )
    table, pair_pull = jax.vjp(
        pair_table,
        pair_embed.astype(jnp.float32),
        pair_gain.astype(jnp.float32),
        pair_weight.astype(jnp.float32),
    )
    squashed = jax.nn.silu(condition.astype(jnp.float32)).astype(jnp.bfloat16)
    modulation = jnp.dot(squashed, full_ada, preferred_element_type=jnp.float32)
    shift_one, scale_one, gate_one, shift_two, scale_two, gate_two = jnp.split(
        modulation[:, None, :], 6, axis=-1
    )
    hidden = hidden_in.astype(jnp.float32)
    first_norm, first_inv = layer_norm(hidden)
    first = (first_norm * (1.0 + scale_one) + shift_one).astype(jnp.bfloat16)
    merged = jnp.einsum("ird,de->ire", first, full_qkv, preferred_element_type=jnp.float32).astype(
        jnp.bfloat16
    )
    queries, keys, values = jnp.split(merged, 3, axis=-1)
    queries4 = queries.reshape(items, rows, H, DH)
    query_pos = lax.axis_index("seq") * rows + jnp.arange(rows, dtype=jnp.int32)
    start_state = (
        jnp.full((items, H, rows), -1e30, jnp.float32),
        jnp.zeros((items, H, rows), jnp.float32),
        jnp.zeros((items, H, rows, DH), jnp.float32),
    )
    carry = start_state
    start = jnp.int32(0)
    key_piece = lax.all_gather(keys, "seq", axis=1, tiled=True)
    value_piece = lax.all_gather(values, "seq", axis=1, tiled=True)
    length = key_piece.shape[1]
    for attend_block in range(length // rows):
        attend_key_block = key_piece[:, attend_block * rows : (attend_block + 1) * rows]
        attend_value_block = value_piece[:, attend_block * rows : (attend_block + 1) * rows]
        attend_key_pos = start + attend_block * rows + jnp.arange(rows, dtype=jnp.int32)
        attend_logits, attend_alive, _ = score_block(
            queries4, attend_key_block, table, query_pos, attend_key_pos, chain_break, valid_len
        )
        run_max, run_sum, accum = carry
        new_max = jnp.maximum(run_max, jnp.max(attend_logits, axis=-1))
        factor = jnp.exp(run_max - new_max)
        attend_probs = jnp.where(attend_alive, jnp.exp(attend_logits - new_max[..., None]), 0.0)
        attend_value4 = attend_value_block.reshape(items, rows, H, DH)
        accum = accum * factor[..., None] + jnp.einsum(
            "ihrn,inhd->ihrd",
            attend_probs.astype(jnp.bfloat16),
            attend_value4,
            preferred_element_type=jnp.float32,
        )
        carry = (new_max, run_sum * factor + jnp.sum(attend_probs, axis=-1), accum)
    run_max, run_sum, accum = carry
    attn_full = accum / run_sum[..., None]
    log_total = run_max + jnp.log(run_sum)
    mixed = jnp.transpose(attn_full, (0, 2, 1, 3)).reshape(items, rows, width).astype(jnp.bfloat16)
    branch = jnp.einsum("ire,ed->ird", mixed, full_out, preferred_element_type=jnp.float32)
    middle = hidden + gate_one * branch
    second_norm, second_inv = layer_norm(middle)
    second = (second_norm * (1.0 + scale_two) + shift_two).astype(jnp.bfloat16)
    gate_up = jnp.einsum("ird,de->ire", second, full_gate_up, preferred_element_type=jnp.float32)
    gate_part, up_part = jnp.split(gate_up, 2, axis=-1)
    inner = (jax.nn.silu(gate_part) * up_part).astype(jnp.bfloat16)
    feed = jnp.einsum("irf,fd->ird", inner, full_down, preferred_element_type=jnp.float32)
    result = (middle + gate_two * feed).astype(jnp.bfloat16)
    upstream = out_grad.astype(jnp.float32)
    feed_grad = (gate_two * upstream).astype(jnp.bfloat16)
    d_gate_two = jnp.sum(upstream * feed, axis=1)
    grad_down = jnp.einsum("irf,ird->fd", inner, feed_grad, preferred_element_type=jnp.float32)
    inner_grad = jnp.einsum("ird,fd->irf", feed_grad, full_down, preferred_element_type=jnp.float32)
    sigmoid_gate = jax.nn.sigmoid(gate_part)
    gate_grad = inner_grad * up_part * sigmoid_gate * (1.0 + gate_part * (1.0 - sigmoid_gate))
    up_grad = inner_grad * gate_part * sigmoid_gate
    gate_up_grad = jnp.concatenate([gate_grad, up_grad], axis=-1).astype(jnp.bfloat16)
    grad_gate_up = jnp.einsum(
        "ird,ire->de", second, gate_up_grad, preferred_element_type=jnp.float32
    )
    second_grad = jnp.einsum(
        "ire,de->ird", gate_up_grad, full_gate_up, preferred_element_type=jnp.float32
    )
    d_shift_two = jnp.sum(second_grad, axis=1)
    d_scale_two = jnp.sum(second_grad * second_norm, axis=1)
    middle_grad = upstream + norm_back(second_grad * (1.0 + scale_two), second_norm, second_inv)
    branch_grad = (gate_one * middle_grad).astype(jnp.bfloat16)
    d_gate_one = jnp.sum(middle_grad * branch, axis=1)
    grad_out = jnp.einsum("ire,ird->ed", mixed, branch_grad, preferred_element_type=jnp.float32)
    mixed_grad = jnp.einsum(
        "ird,ed->ire", branch_grad, full_out, preferred_element_type=jnp.float32
    ).astype(jnp.bfloat16)
    mixed_grad4 = mixed_grad.reshape(items, rows, H, DH)
    delta = jnp.einsum(
        "irhd,ihrd->ihr", mixed_grad4.astype(jnp.float32), attn_full, precision=HIGHEST
    )
    all_keys, all_values = (
        lax.all_gather(keys, "seq", axis=1, tiled=True),
        lax.all_gather(values, "seq", axis=1, tiled=True),
    )
    query_grad = jnp.zeros((items, rows, H, DH), jnp.float32)
    table_grad = jnp.zeros((CLASSES, H), jnp.float32)
    key_terms = []
    value_terms = []
    class_range = jnp.arange(CLASSES, dtype=jnp.int32)
    for block in range(seq_count):
        key_block = all_keys[:, block * rows : (block + 1) * rows]
        value_block = all_values[:, block * rows : (block + 1) * rows]
        key_pos = block * rows + jnp.arange(rows, dtype=jnp.int32)
        logits, alive, classes = score_block(
            queries4, key_block, table, query_pos, key_pos, chain_break, valid_len
        )
        probs = jnp.where(alive, jnp.exp(logits - log_total[..., None]), 0.0)
        key4 = key_block.reshape(items, rows, H, DH)
        value4 = value_block.reshape(items, rows, H, DH)
        prob_grad = jnp.einsum(
            "irhd,inhd->ihrn", mixed_grad4, value4, preferred_element_type=jnp.float32
        )
        score_grad = (probs * (prob_grad - delta[..., None])).astype(jnp.bfloat16)
        query_grad = (
            query_grad
            + jnp.einsum("ihrn,inhd->irhd", score_grad, key4, preferred_element_type=jnp.float32)
            * 0.125
        )
        key_terms.append(
            (
                jnp.einsum(
                    "ihrn,irhd->inhd", score_grad, queries4, preferred_element_type=jnp.float32
                )
                * 0.125
            ).reshape(items, rows, width)
        )
        value_terms.append(
            jnp.einsum(
                "ihrn,irhd->inhd",
                probs.astype(jnp.bfloat16),
                mixed_grad4,
                preferred_element_type=jnp.float32,
            ).reshape(items, rows, width)
        )
        one_hot = (classes[..., None] == class_range).astype(jnp.bfloat16)
        table_grad = table_grad + jnp.einsum(
            "ihrn,irnc->ch", score_grad, one_hot, preferred_element_type=jnp.float32
        )
    key_grad, value_grad = (
        lax.psum_scatter(
            jnp.concatenate(key_terms, axis=1).astype(jnp.bfloat16),
            "seq",
            scatter_dimension=1,
            tiled=True,
        ).astype(jnp.float32),
        lax.psum_scatter(
            jnp.concatenate(value_terms, axis=1).astype(jnp.bfloat16),
            "seq",
            scatter_dimension=1,
            tiled=True,
        ).astype(jnp.float32),
    )
    merged_grad = jnp.concatenate(
        [query_grad.reshape(items, rows, width), key_grad, value_grad], axis=-1
    ).astype(jnp.bfloat16)
    grad_qkv = jnp.einsum("ird,ire->de", first, merged_grad, preferred_element_type=jnp.float32)
    first_grad = jnp.einsum(
        "ire,de->ird", merged_grad, full_qkv, preferred_element_type=jnp.float32
    )
    d_shift_one = jnp.sum(first_grad, axis=1)
    d_scale_one = jnp.sum(first_grad * first_norm, axis=1)
    input_grad = middle_grad + norm_back(first_grad * (1.0 + scale_one), first_norm, first_inv)
    modulation_grad = jnp.concatenate(
        [d_shift_one, d_scale_one, d_gate_one, d_shift_two, d_scale_two, d_gate_two], axis=-1
    )
    grad_ada = jnp.einsum(
        "ic,ie->ce", squashed.astype(jnp.float32), modulation_grad, precision=HIGHEST
    )
    table_total = lax.psum(table_grad, ("dp", "seq"))
    grad_embed, grad_gain, grad_pair = pair_pull(table_total)
    local_grads = (grad_qkv, grad_out, grad_gate_up, grad_down, grad_ada)
    shares = (
        lax.psum_scatter(
            local_grads[0].astype(jnp.bfloat16), "dp", scatter_dimension=0, tiled=True
        ).astype(jnp.float32),
        lax.psum_scatter(
            local_grads[1].astype(jnp.bfloat16), "dp", scatter_dimension=0, tiled=True
        ).astype(jnp.float32),
        lax.psum_scatter(
            local_grads[2].astype(jnp.bfloat16), "dp", scatter_dimension=0, tiled=True
        ).astype(jnp.float32),
        lax.psum_scatter(
            local_grads[3].astype(jnp.bfloat16), "dp", scatter_dimension=0, tiled=True
        ).astype(jnp.float32),
        lax.psum_scatter(
            local_grads[4].astype(jnp.bfloat16), "dp", scatter_dimension=0, tiled=True
        ).astype(jnp.float32),
    )
    reduced = (
        lax.psum(shares[0].astype(jnp.bfloat16), "seq").astype(jnp.float32),
        lax.psum(shares[1].astype(jnp.bfloat16), "seq").astype(jnp.float32),
        lax.psum(shares[2].astype(jnp.bfloat16), "seq").astype(jnp.float32),
        lax.psum(shares[3].astype(jnp.bfloat16), "seq").astype(jnp.float32),
        lax.psum(shares[4].astype(jnp.bfloat16), "seq").astype(jnp.float32),
    )
    return (
        result,
        input_grad.astype(jnp.bfloat16),
        reduced[0],
        reduced[1],
        reduced[2],
        reduced[3],
        reduced[4],
        grad_embed,
        grad_gain,
        grad_pair,
    )


def solution(mesh):
    return jax.shard_map(
        body,
        mesh=mesh,
        in_specs=(
            P("dp", "seq", None),
            P("dp", None),
            P("dp", None),
            P("dp", None),
            P("dp", None),
            P("dp", None),
            P("dp", None),
            P(),
            P(),
            P(),
            P("dp"),
            P("dp"),
            P("dp", "seq", None),
        ),
        out_specs=(
            P("dp", "seq", None),
            P("dp", "seq", None),
            P("dp", None),
            P("dp", None),
            P("dp", None),
            P("dp", None),
            P("dp", None),
            P(),
            P(),
            P(),
        ),
        check_vma=False,
    )
```

profile of v0, /device:TPU:0, one launch (start us, length us, event | category | flops | bytes accessed | tf_op | source)
XLA Modules:
  0.0 1803.8 jit_solution(8868757937583857605)
XLA Ops:
  11.1 53.9 %all-gather.8.cloned.1.call-done = bf16[256,4608]{1,0:T(8,128)(2,1)} async-done(((bf16[32,4608]{1,0:T(8,128)(2,1)}), bf16[256,4608]{1,0:T(8,128)(2,1)}) %all-gather.8.cloned.1.call-update) | async-done | bytes 2359312 | tf_op jit(solution)/shard_map/all_gather | solution.py:76
  67.8 63.2 %all-gather.10.cloned.1.call-done = bf16[768,2304]{1,0:T(8,128)(2,1)} async-done(((bf16[96,2304]{1,0:T(8,128)(2,1)}), bf16[768,2304]{1,0:T(8,128)(2,1)}) %all-gather.10.cloned.1.call-update) | async-done | bytes 3538960 | tf_op jit(solution)/shard_map/all_gather | solution.py:72
  143.7 217.1 %gather_fusion = f32[65536,12]{1,0:T(8,128)} fusion(f32[66,12]{1,0:T(8,128)S(1)} %fusion.198, s32[65536]{0:T(1024)S(1)} %broadcast_clamp_fusion.3), kind=kCustom, calls=%fused_computation.clone | custom fusion | bytes 6553600 | tf_op jit(solution)/shard_map/jit(_take)/gather | solution.py:49
  360.8 20.6 %copy.88 = f32[1,256,256,12]{1,2,3,0:T(8,128)} copy(f32[1,256,256,12]{3,2,1,0:T(8,128)} %bitcast.349) | data formatting | bytes 6291456 | tf_op jit(solution)/shard_map/jit(_take)/gather | solution.py:49
  383.0 217.1 %gather_fusion.2 = f32[65536,12]{1,0:T(8,128)} fusion(f32[66,12]{1,0:T(8,128)S(1)} %fusion.198, s32[65536]{0:T(1024)S(1)} %broadcast_clamp_fusion.1), kind=kCustom, calls=%fused_computation.2.clone | custom fusion | bytes 6553600 | tf_op jit(solution)/shard_map/jit(_take)/gather | solution.py:49
  600.1 20.4 %copy.102 = f32[1,256,256,12]{1,2,3,0:T(8,128)} copy(f32[1,256,256,12]{3,2,1,0:T(8,128)} %bitcast.350) | data formatting | bytes 6291456 | tf_op jit(solution)/shard_map/jit(_take)/gather | solution.py:49
  621.4 217.1 %gather_fusion.1 = f32[65536,12]{1,0:T(8,128)} fusion(f32[66,12]{1,0:T(8,128)S(1)} %fusion.198, s32[65536]{0:T(1024)S(1)} %broadcast_clamp_fusion.2), kind=kCustom, calls=%fused_computation.1.clone | custom fusion | bytes 6553600 | tf_op jit(solution)/shard_map/jit(_take)/gather | solution.py:49
  838.5 20.3 %copy.95 = f32[1,256,256,12]{1,2,3,0:T(8,128)} copy(f32[1,256,256,12]{3,2,1,0:T(8,128)} %bitcast.351) | data formatting | bytes 6291456 | tf_op jit(solution)/shard_map/jit(_take)/gather | solution.py:49
  859.8 217.1 %gather_fusion.3 = f32[65536,12]{1,0:T(8,128)} fusion(f32[66,12]{1,0:T(8,128)S(1)} %fusion.198, s32[65536]{0:T(1024)S(1)} %broadcast_clamp_fusion), kind=kCustom, calls=%fused_computation.3.clone | custom fusion | bytes 6553600 | tf_op jit(solution)/shard_map/jit(_take)/gather | solution.py:49
  1076.9 20.5 %copy.109 = f32[1,256,256,12]{1,2,3,0:T(8,128)} copy(f32[1,256,256,12]{3,2,1,0:T(8,128)} %bitcast.348) | data formatting | bytes 6291456 | tf_op jit(solution)/shard_map/jit(_take)/gather | solution.py:49
  1134.7 9.8 convolution_bitcast_fusion
  1144.5 7.9 fusion.86
  1152.4 6.3 fusion.171
  1159.4 5.6 fusion.170
  1197.9 10.5 reduce-scatter.8.cloned.1.call-done
  1208.5 31.5 %reduce-scatter.10.cloned.1.call-done = bf16[1,256,768]{1,2,0:T(8,128)(2,1)} async-done(((bf16[1,1024,768]{1,2,0:T(8,128)(2,1)}), bf16[1,256,768]{1,2,0:T(8,128)(2,1)}) %reduce-scatter.10.cloned.1.call-update) | async-done | bytes 393232 | tf_op jit(solution)/shard_map/reduce_scatter | solution.py:223
  1253.3 5.2 convolution_convert_fusion.1
  1263.0 8.7 convolution_convert_fusion
  1288.7 39.5 %psum.47 = f32[66,12]{0,1:T(8,128)S(1)} all-reduce(f32[66,12]{0,1:T(8,128)S(1)} %fusion.148), channel_id=1, replica_groups=mesh['dp'=8,'seq'=4] {'dp','seq'}, use_global_device_ids=true, to_apply=%region_36.38 | all-reduce | flops 792 | bytes 6336 | tf_op jit(solution)/shard_map/psum | solution.py:246
  1329.3 51.0 %reduce-scatter.20.cloned.1.call-done = bf16[32,4608]{1,0:T(8,128)(2,1)} async-done(((bf16[256,4608]{1,0:T(8,128)(2,1)}), bf16[32,4608]{1,0:T(8,128)(2,1)}) %reduce-scatter.20.cloned.1.call-update) | async-done | bytes 294928 | tf_op jit(solution)/shard_map/reduce_scatter | solution.py:262
  1380.3 98.0 %reduce-scatter.18.cloned.1.call-done = bf16[384,768]{1,0:T(8,128)(2,1)} async-done(((bf16[3072,768]{1,0:T(8,128)(2,1)}), bf16[384,768]{1,0:T(8,128)(2,1)}) %reduce-scatter.18.cloned.1.call-update) | async-done | bytes 589840 | tf_op jit(solution)/shard_map/reduce_scatter | solution.py:259
  1478.2 82.5 %reduce-scatter.12.cloned.1.call-done = bf16[96,2304]{1,0:T(8,128)(2,1)} async-done(((bf16[768,2304]{1,0:T(8,128)(2,1)}), bf16[96,2304]{1,0:T(8,128)(2,1)}) %reduce-scatter.12.cloned.1.call-update) | async-done | bytes 442384 | tf_op jit(solution)/shard_map/reduce_scatter | solution.py:250
  1560.8 166.5 %reduce-scatter.16.cloned.1.call-done = bf16[96,6144]{1,0:T(8,128)(2,1)} async-done(((bf16[768,6144]{1,0:T(8,128)(2,1)}), bf16[96,6144]{1,0:T(8,128)(2,1)}) %reduce-scatter.16.cloned.1.call-update) | async-done | bytes 1179664 | tf_op jit(solution)/shard_map/reduce_scatter | solution.py:256
  1730.0 60.1 %all-reduce.3.cloned.1.call-done = (bf16[96,2304]{1,0:T(8,128)(2,1)}, bf16[96,768]{1,0:T(8,128)(2,1)}, bf16[96,6144]{1,0:T(8,128)(2,1)}, bf16[384,768]{1,0:T(8,128)(2,1)}, bf16[32,4608]{1,0:T(8,128)(2,1)}) async-done(((bf16[96,2304]{1,0:T(8,128)(2,1)}, bf16[96,768]{1,0:T(8,128)(2,1)}, bf16[96,6144]{1,0:T(8,128)(2,1)}, bf16[384,768]{1,0:T(8,128)(2,1)}, bf16[32,4608]{1,0:T(8,128)(2,1)}), ...) | async-done | bytes 2654224 | tf_op jit(solution)/shard_map/psum | solution.py:267
  (395 shorter events, 136.4 us)
Async XLA Ops:
  7.2 136.3 %copy-start = (bf16[256,12]{0,1:T(8,128)(2,1)S(1)}, bf16[256,12]{0,1:T(8,128)(2,1)}, u32[]{:S(2)}) copy-start(bf16[256,12]{0,1:T(8,128)(2,1)} %param.24) | copy-start | bytes 18436
  7.2 57.8 %all-gather.8.cloned.1.call-start = ((), (), s32[]{:S(2)}) async-start(), calls=%async_computation.7 | async-start | bytes 2654208 | tf_op jit(solution)/shard_map/all_gather | solution.py:76
  7.9 123.0 %all-gather.10.cloned.1.call-start = ((), (), s32[]{:S(2)}) async-start(), calls=%async_computation.8 | async-start | bytes 3981312 | tf_op jit(solution)/shard_map/all_gather | solution.py:72
  8.7 1090.3 %all-gather.12.cloned.1.call-start = ((), (), s32[]{:S(2)}) async-start(), calls=%async_computation.9 | async-start | bytes 1966080 | tf_op jit(solution)/shard_map/all_gather | solution.py:105
  9.9 124.3 %copy-start.96 = (f32[256]{0:T(256)}, f32[256]{0:T(256)S(1)}, u32[]{:S(2)}) copy-start(f32[256]{0:T(256)S(1)} %broadcast_multiply_fusion.5) | copy-start | bytes 3076
  135.2 969.0 %all-gather.14.cloned.1.call-start = ((), (), s32[]{:S(2)}) async-start(), calls=%async_computation.10 | async-start | bytes 1966080 | tf_op jit(solution)/shard_map/all_gather | solution.py:106
  135.8 994.3 %all-gather.16.cloned.1.call-start = ((), (), s32[]{:S(2)}) async-start(), calls=%async_computation.11 | async-start | bytes 1327104 | tf_op jit(solution)/shard_map/all_gather | solution.py:73
  136.4 998.2 %all-gather.18.cloned.1.call-start = ((), (), s32[]{:S(2)}) async-start(), calls=%async_computation.12 | async-start | bytes 10616832 | tf_op jit(solution)/shard_map/all_gather | solution.py:74
  137.0 1007.5 %all-gather.20.cloned.1.call-start = ((), (), s32[]{:S(2)}) async-start(), calls=%async_computation.13 | async-start | bytes 5308416 | tf_op jit(solution)/shard_map/all_gather | solution.py:75
  137.7 1070.7 %reduce-scatter.8.cloned.1.call-start = ((), (), s32[]{:S(2)}) async-start(), calls=%async_computation.14 | async-start | bytes 1966080 | tf_op jit(solution)/shard_map/reduce_scatter | solution.py:217
  1181.7 58.2 %reduce-scatter.10.cloned.1.call-start = ((), (), s32[]{:S(2)}) async-start(), calls=%async_computation.15 | async-start | bytes 1966080 | tf_op jit(solution)/shard_map/reduce_scatter | solution.py:223
  1189.0 140.3 %reduce-scatter.14.cloned.1.call-start = ((), (), s32[]{:S(2)}) async-start(), calls=%async_computation.17 | async-start | bytes 1327104 | tf_op jit(solution)/shard_map/reduce_scatter | solution.py:253
  1197.9 182.4 %reduce-scatter.20.cloned.1.call-start = ((), (), s32[]{:S(2)}) async-start(), calls=%async_computation.20 | async-start | bytes 2654208 | tf_op jit(solution)/shard_map/reduce_scatter | solution.py:262
  1253.2 225.0 %reduce-scatter.18.cloned.1.call-start = ((), (), s32[]{:S(2)}) async-start(), calls=%async_computation.19 | async-start | bytes 5308416 | tf_op jit(solution)/shard_map/reduce_scatter | solution.py:259
  1258.5 302.3 %reduce-scatter.12.cloned.1.call-start = ((), (), s32[]{:S(2)}) async-start(), calls=%async_computation.16 | async-start | bytes 3981312 | tf_op jit(solution)/shard_map/reduce_scatter | solution.py:250
  1262.9 464.3 %reduce-scatter.16.cloned.1.call-start = ((), (), s32[]{:S(2)}) async-start(), calls=%async_computation.18 | async-start | bytes 10616832 | tf_op jit(solution)/shard_map/reduce_scatter | solution.py:256
  1271.7 518.4 %all-reduce.3.cloned.1.call-start = ((), (), s32[]{:S(2)}) async-start(), calls=%async_computation.21 | async-start | bytes 5308416 | tf_op jit(solution)/shard_map/psum | solution.py:267
  1288.7 440.2 %copy-start.108 = (f32[256]{0:T(256)S(1)}, f32[256]{0:T(256)}, u32[]{:S(2)}) copy-start(f32[256]{0:T(256)} %get-tuple-element.18) | copy-start | bytes 3076
  1288.7 440.2 %copy-start.115 = (f32[256]{0:T(256)S(1)}, f32[256]{0:T(256)}, u32[]{:S(2)}) copy-start(f32[256]{0:T(256)} %get-tuple-element.14) | copy-start | bytes 3076
  1288.7 440.2 %copy-start.27 = (f32[1,256,768]{2,1,0:T(8,128)S(1)}, f32[1,256,768]{2,1,0:T(8,128)}, u32[]{:S(2)}) copy-start(f32[1,256,768]{2,1,0:T(8,128)} %copy-done.25) | copy-start | bytes 2359300
  1288.7 440.2 %copy-start.46 = (f32[256,768]{1,0:T(8,128)S(1)}, f32[256,768]{1,0:T(8,128)}, u32[]{:S(2)}) copy-start(f32[256,768]{1,0:T(8,128)} %copy-done.45) | copy-start | bytes 2359300
  1288.7 440.2 %copy-start.76 = (f32[768]{0:T(1024)S(1)}, f32[768]{0:T(1024)}, u32[]{:S(2)}) copy-start(f32[768]{0:T(1024)} %copy-done.74) | copy-start | bytes 9220
  1288.7 440.2 %copy-start.97 = (f32[256]{0:T(256)S(1)}, f32[256]{0:T(256)}, u32[]{:S(2)}) copy-start(f32[256]{0:T(256)} %copy-done.96) | copy-start | bytes 3076
  1288.7 440.2 %copy-start.107 = (f32[256]{0:T(256)S(1)}, f32[256]{0:T(256)}, u32[]{:S(2)}) copy-start(f32[256]{0:T(256)} %copy-done.106) | copy-start | bytes 3076
  (110 other events, 1194.7 us)
Sparse Core Ops, SparseCore 0:
  10.2 54.7 all-gather.7
  67.2 63.7 all-gather.9
  135.4 18.1 all-gather.11
  155.5 19.6 all-gather.13
  177.3 41.0 all-gather.15
  220.4 136.8 all-gather.17
  359.4 78.0 all-gather.19
  1181.9 26.5 reduce-scatter.7
  1211.7 28.1 reduce-scatter.9
  1243.8 64.0 reduce-scatter.13
  1311.9 68.2 reduce-scatter.19
  1383.8 94.4 reduce-scatter.17
  1481.9 78.8 reduce-scatter.11
  1564.2 162.9 reduce-scatter.15
  1729.8 60.2 all-reduce.2
where the time goes:
time: 1810 us; the launch traced here: 1800 us
  local copies, waits for them, and re-layouts  986 us (54%)
  waiting for transfers between devices  621 us (34%)
  matrix products  107 us (6%)
  blocking collectives  39.5 us (2%)
  other arithmetic  31.5 us (2%)
    gather x8, local copies, waits for them, and re-layouts, score_block(): bias = jnp.moveaxis(jnp.take(table, classes, axis=0), -1, 1)  950 us
    reduce_scatter x1, waiting for transfers between devices, body(): lax.psum_scatter(local_grads[2].astype(jnp.bfloat16), 'dp', scatter_dimen...  166 us
    reduce_scatter x1, waiting for transfers between devices, body(): lax.psum_scatter(local_grads[3].astype(jnp.bfloat16), 'dp', scatter_dimen...  98 us
    reduce_scatter x1, waiting for transfers between devices, body(): lax.psum_scatter(local_grads[0].astype(jnp.bfloat16), 'dp', scatter_dimen...  82.5 us
    all_gather x1, waiting for transfers between devices, body(): lax.all_gather(qkv_weight, 'dp', axis=0, tiled=True)  63.2 us
    psum x1, waiting for transfers between devices, body(): lax.psum(shares[0].astype(jnp.bfloat16), 'seq').astype(jnp.float32)  60.1 us
    all_gather x1, waiting for transfers between devices, body(): lax.all_gather(ada_weight, 'dp', axis=0, tiled=True)  53.9 us
    reduce_scatter x1, waiting for transfers between devices, body(): lax.psum_scatter(local_grads[4].astype(jnp.bfloat16), 'dp', scatter_dimen...  51 us
  transfers between devices with their start and end apart: 15, of which 9 were waited for; matrix products, arithmetic and copies ran while one was open for 59% of the time, Pallas kernels for 0%

commit v1 on v0

v1 whole, which is shorter than its diff:
```python
import jax
import jax.numpy as jnp
from jax import lax
from jax.sharding import PartitionSpec as P

H = 12
DH = 64
RR = 32
CLASSES = 66

HIGHEST = lax.Precision.HIGHEST
F32 = jnp.float32
BF16 = jnp.bfloat16


def layer_norm(values):
    average = jnp.mean(values, axis=-1, keepdims=True)
    centered = values - average
    inv_std = lax.rsqrt(jnp.mean(centered * centered, axis=-1, keepdims=True) + 1e-06)
    return (centered * inv_std, inv_std)


def norm_back(upstream, normal, inv_std):
    return inv_std * (
        upstream
        - jnp.mean(upstream, axis=-1, keepdims=True)
        - normal * jnp.mean(upstream * normal, axis=-1, keepdims=True)
    )


def pair_table(pair_embed, pair_gain, pair_weight):
    average = jnp.mean(pair_embed, axis=-1, keepdims=True)
    centered = pair_embed - average
    normal = centered * lax.rsqrt(jnp.mean(centered * centered, axis=-1, keepdims=True) + 1e-05)
    return jnp.dot(normal * pair_gain, pair_weight, precision=HIGHEST)


def mm(spec, a, b):
    return jnp.einsum(spec, a, b, preferred_element_type=F32)


def body(
    hidden_in,
    condition,
    qkv_weight,
    out_weight,
    gate_up_weight,
    down_weight,
    ada_weight,
    pair_embed,
    pair_gain,
    pair_weight,
    valid_len,
    chain_break,
    out_grad,
):
    items, rows, width = hidden_in.shape
    seq = lax.axis_size("seq")
    dp = lax.axis_size("dp")
    me = lax.axis_index("seq")
    at = lax.axis_index("dp")
    length = rows * seq
    heads = H // seq
    part = heads * DH
    shard = qkv_weight.shape[0]
    strip = down_weight.shape[0] // seq
    hidden_units = dp * strip

    def pick(array, axis):
        return lax.dynamic_index_in_dim(array, me, axis, keepdims=False)

    def gather(array, name, axis):
        return lax.all_gather(array, name, axis=axis, tiled=True)

    def scatter(array, name, axis):
        return lax.psum_scatter(array, name, scatter_dimension=axis, tiled=True)

    conditions = gather(condition, "dp", 0)
    squashed = jax.nn.silu(conditions.astype(F32)).astype(BF16)
    ada_rows = ada_weight.shape[0]
    squashed_part = lax.dynamic_slice_in_dim(squashed, at * ada_rows, ada_rows, 1)
    modulation = scatter(mm("ic,ce->ie", squashed_part, ada_weight), "dp", 0)
    shift_one, scale_one, gate_one, shift_two, scale_two, gate_two = jnp.split(
        modulation[:, None, :], 6, axis=-1
    )
    qkv_w = gather(pick(qkv_weight.reshape(shard, 3, seq, part), 2).reshape(shard, 3 * part), "dp", 0)
    gate_up_w = gather(
        pick(gate_up_weight.reshape(shard, 2, dp, seq, strip), 3).reshape(shard, 2 * hidden_units), "dp", 0
    )
    down_w = gather(pick(down_weight.reshape(seq, strip, width), 0), "dp", 0)
    out_w = gather(gather(pick(out_weight.reshape(shard, seq, width // seq), 1), "dp", 0), "seq", 1)

    table, pair_pull = jax.vjp(
        pair_table, pair_embed.astype(F32), pair_gain.astype(F32), pair_weight.astype(F32)
    )
    my_table = lax.dynamic_slice_in_dim(table, me * heads, heads, 1)
    spread = jnp.arange(2 * length)
    distance = jnp.where(spread < length, -spread, 2 * length - spread)
    line = jnp.take(my_table, jnp.clip(distance, -RR, RR) + RR, axis=0).T
    toeplitz = jnp.tile(line, (1, length))[:, : length * (2 * length - 1)]
    toeplitz = toeplitz.reshape(heads, length, 2 * length - 1)[:, :, :length]
    positions = jnp.arange(length, dtype=jnp.int32)
    side = positions[None] >= chain_break[:, None]
    same = side[:, :, None] == side[:, None, :]
    alive = (positions[None] < valid_len[:, None])[:, None, None, :]

    hidden = gather(hidden_in, "seq", 1).astype(F32)
    upstream = out_grad.astype(F32)
    first_norm, first_inv = layer_norm(hidden)
    first = (first_norm * (1.0 + scale_one) + shift_one).astype(BF16)
    merged = mm("ird,de->ire", first, qkv_w).astype(BF16)
    queries, keys, values = (
        part_of.reshape(items, length, heads, DH) for part_of in jnp.split(merged, 3, axis=-1)
    )
    logits = mm("iqhd,ikhd->ihqk", queries, keys) * 0.125
    logits = logits + jnp.where(same[:, None], toeplitz[None], my_table[CLASSES - 1][None, :, None, None])
    logits = jnp.where(alive, logits, -1e30)
    powers = jnp.exp(logits - jnp.max(logits, axis=-1, keepdims=True))
    probs = powers / jnp.sum(powers, axis=-1, keepdims=True)
    probs_low = probs.astype(BF16)
    mixed_heads = mm("ihqk,ikhd->iqhd", probs_low, values)
    mixed_part = mixed_heads.reshape(items, length, part).astype(BF16)
    mixed_all = gather(mixed_part, "seq", 2)

    def mine(array):
        return lax.dynamic_slice_in_dim(array, me * rows, rows, 1)

    branch = mm("ire,ed->ird", mine(mixed_all), out_w)
    middle = hidden_in.astype(F32) + gate_one * branch
    second_norm, second_inv = layer_norm(middle)
    second = gather((second_norm * (1.0 + scale_two) + shift_two).astype(BF16), "seq", 1)
    gate_up = mm("ird,de->ire", second, gate_up_w)
    gate_part, up_part = jnp.split(gate_up, 2, axis=-1)
    sigmoid_gate = jax.nn.sigmoid(gate_part)
    inner = (gate_part * sigmoid_gate * up_part).astype(BF16)
    feed = scatter(mm("irf,fd->ird", inner, down_w).astype(BF16), "seq", 1).astype(F32)
    result = (middle + gate_two * feed).astype(BF16)

    feed_grad = (gate_two * gather(out_grad, "seq", 1).astype(F32)).astype(BF16)
    d_gate_two = jnp.sum(upstream * feed, axis=1)
    grad_down = mm("irf,ird->fd", inner, feed_grad)
    inner_grad = mm("ird,fd->irf", feed_grad, down_w)
    gate_grad = inner_grad * up_part * sigmoid_gate * (1.0 + gate_part * (1.0 - sigmoid_gate))
    up_grad = inner_grad * gate_part * sigmoid_gate
    gate_up_grad = jnp.concatenate([gate_grad, up_grad], axis=-1).astype(BF16)
    grad_gate_up = mm("ird,ire->de", second, gate_up_grad)
    second_grad = scatter(mm("ire,de->ird", gate_up_grad, gate_up_w).astype(BF16), "seq", 1).astype(F32)
    d_shift_two = jnp.sum(second_grad, axis=1)
    d_scale_two = jnp.sum(second_grad * second_norm, axis=1)
    middle_grad = upstream + norm_back(second_grad * (1.0 + scale_two), second_norm, second_inv)
    branch_grad = (gate_one * middle_grad).astype(BF16)
    d_gate_one = jnp.sum(middle_grad * branch, axis=1)
    branch_grad_all = gather(branch_grad, "seq", 1)
    my_columns = lax.dynamic_slice_in_dim(branch_grad_all, me * part, part, 2)
    grad_out = mm("ire,ird->ed", mixed_all, my_columns)
    out_w_rows = lax.dynamic_slice_in_dim(out_w, me * part, part, 0)
    mixed_grad = mm("ird,ed->ire", branch_grad_all, out_w_rows).astype(BF16).reshape(items, length, heads, DH)

    prob_grad = mm("iqhd,ikhd->ihqk", mixed_grad, values)
    delta = jnp.sum(probs * prob_grad, axis=-1, keepdims=True)
    score_grad = (probs * (prob_grad - delta)).astype(BF16)
    query_grad = mm("ihqk,ikhd->iqhd", score_grad, keys) * 0.125
    key_grad = mm("ihqk,iqhd->ikhd", score_grad, queries) * 0.125
    value_grad = mm("ihqk,iqhd->ikhd", probs_low, mixed_grad)
    merged_grad = jnp.concatenate(
        [term.reshape(items, length, part) for term in (query_grad, key_grad, value_grad)], axis=-1
    ).astype(BF16)
    wide = score_grad.astype(F32)
    kept = jnp.sum(jnp.where(same[:, None], wide, 0.0), axis=0)
    crossed = jnp.sum(jnp.where(same[:, None], 0.0, wide), axis=(0, 2, 3))
    skewed = jnp.pad(kept[:, :, ::-1], ((0, 0), (0, 0), (0, length))).reshape(heads, -1)
    skewed = skewed[:, : length * (2 * length - 1)].reshape(heads, length, 2 * length - 1)
    lines = jnp.sum(skewed, axis=1)
    middle_line = length - 1
    low_end = jnp.sum(lines[:, : middle_line - RR + 1], axis=1)
    high_end = jnp.sum(lines[:, middle_line + RR :], axis=1)
    near = lines[:, middle_line - RR + 1 : middle_line + RR]
    my_table_grad = jnp.concatenate([low_end[:, None], near, high_end[:, None], crossed[:, None]], axis=1).T
    table_grad = lax.psum(
        lax.dynamic_update_slice_in_dim(jnp.zeros((CLASSES, H), F32), my_table_grad, me * heads, 1), ("dp", "seq")
    )
    grad_embed, grad_gain, grad_pair = pair_pull(table_grad)

    grad_qkv = mm("ird,ire->de", first, merged_grad)
    first_grad = scatter(mm("ire,de->ird", merged_grad, qkv_w).astype(BF16), "seq", 1).astype(F32)
    my_norm, my_inv = mine(first_norm), mine(first_inv)
    d_shift_one = jnp.sum(first_grad, axis=1)
    d_scale_one = jnp.sum(first_grad * my_norm, axis=1)
    input_grad = middle_grad + norm_back(first_grad * (1.0 + scale_one), my_norm, my_inv)
    modulation_grad = jnp.concatenate(
        [d_shift_one, d_scale_one, d_gate_one, d_shift_two, d_scale_two, d_gate_two], axis=-1
    )
    modulation_grads = gather(lax.psum(modulation_grad, "seq"), "dp", 0)
    grad_ada = jnp.einsum("ic,ie->ce", squashed_part.astype(F32), modulation_grads, precision=HIGHEST)

    def owned(grad):
        return scatter(grad.astype(BF16), "dp", 0)

    def everyone(grad):
        return lax.all_gather(grad, "seq", axis=0)

    shares_qkv = everyone(owned(grad_qkv)).reshape(seq, shard, 3, part)
    shares_out = everyone(owned(grad_out))
    shares_gate_up = everyone(owned(grad_gate_up)).reshape(seq, shard, 2, dp, strip)
    shares_down = everyone(owned(grad_down))
    return (
        result,
        input_grad.astype(BF16),
        jnp.transpose(shares_qkv, (1, 2, 0, 3)).reshape(shard, -1).astype(F32),
        jnp.transpose(shares_out, (1, 0, 2)).reshape(shard, -1).astype(F32),
        jnp.transpose(shares_gate_up, (1, 2, 3, 0, 4)).reshape(shard, -1).astype(F32),
        shares_down.reshape(seq * strip, width).astype(F32),
        grad_ada,
        grad_embed,
        grad_gain,
        grad_pair,
    )


def solution(mesh):
    rows = P("dp", "seq", None)
    share = P("dp", None)
    return jax.shard_map(
        body,
        mesh=mesh,
        in_specs=(rows, share, share, share, share, share, share, P(), P(), P(), P("dp"), P("dp"), rows),
        out_specs=(rows, rows, share, share, share, share, share, P(), P(), P()),
        check_vma=False,
    )
```

time: 1810 us -> 2050 us (1.13); the launches traced: 1800 us -> 2010 us
  local copies, waits for them, and re-layouts: 986 us -> 1330 us
  waiting for transfers between devices: 621 us -> 299 us
  blocking collectives: 39.5 us -> 192 us
  other arithmetic: 31.5 us -> 66.7 us
    unnamed x247 -> x131, local copies, waits for them, and re-layouts: 14.6 us -> 1100 us
    gather x8 -> x1, local copies, waits for them, and re-layouts: 950 us -> 5.45 us  [body(): line = jnp.take(my_table, jnp.clip(distance, -RR, RR) + RR, axis=0).T]
    reduce_scatter x7, waiting for transfers between devices: 440 us -> 156 us  [scatter(): return lax.psum_scatter(array, name, scatter_dimension=axis, tiled=True)]
    all_gather x0 -> x7, blocking collectives: none -> 141 us  [the longest x4 119 us: gather(): return lax.all_gather(array, name, axis=axis, tiled=True)]
    rev x0 -> x1, local copies, waits for them, and re-layouts: none -> 96 us  [body(): kept[:, :, ::-1]]
    reshape x0 -> x7, local copies, waits for them, and re-layouts: none -> 81.8 us  [the longest x1 37.4 us: body(): toeplitz = toeplitz.reshape(heads, length, 2 * length - 1)[:, :, :length]]
    psum x1 -> x0, waiting for transfers between devices: 60.1 us -> none  [body(): lax.psum(shares[0].astype(jnp.bfloat16), 'seq').astype(jnp.float32)]
    all_gather x7 -> x9, waiting for transfers between devices: 117 us -> 142 us  [the longest x8 142 us: gather(): return lax.all_gather(array, name, axis=axis, tiled=True)]
  transfers between devices with their start and end apart: 15 -> 17, of which waited for: 9 -> 10; matrix products, arithmetic and copies ran while one was open for 59% -> 73% of each run, Pallas kernels for 0% -> 0%
where the time goes in v1:
time: 2050 us; the launch traced here: 2010 us
  local copies, waits for them, and re-layouts  1330 us (65%)
  waiting for transfers between devices  299 us (15%)
  blocking collectives  192 us (9%)
  matrix products  103 us (5%)
  other arithmetic  66.7 us (3%)
    unnamed x131, local copies, waits for them, and re-layouts  1100 us
    reduce_scatter x7, waiting for transfers between devices, scatter(): return lax.psum_scatter(array, name, scatter_dimension=axis, tiled=True)  156 us
    all_gather x8, waiting for transfers between devices, gather(): return lax.all_gather(array, name, axis=axis, tiled=True)  142 us
    all_gather x4, blocking collectives, gather(): return lax.all_gather(array, name, axis=axis, tiled=True)  119 us
    dot_general x19, matrix products, mm(): return jnp.einsum(spec, a, b, preferred_element_type=F32)  100 us
    rev x1, local copies, waits for them, and re-layouts, body(): kept[:, :, ::-1]  96 us
  transfers between devices with their start and end apart: 17, of which 10 were waited for; matrix products, arithmetic and copies ran while one was open for 73% of the time, Pallas kernels for 0%

profile of v1, /device:TPU:0, one launch (start us, length us, event | category | flops | bytes accessed | tf_op | source)
XLA Modules:
  0.0 2012.5 jit_solution(7987416564520951256)
XLA Ops:
  69.2 34.9 %all_gather.62 = bf16[768,576]{1,0:T(8,128)(2,1)} all-gather(bf16[96,576]{1,0:T(8,128)(2,1)S(1)} %copy.109), channel_id=1, replica_groups=mesh['dp'=8,'seq'=4] {'dp'}, dimensions={0}, use_global_device_ids=true | all-gather | bytes 995328 | tf_op jit(solution)/shard_map/all_gather | solution.py:73
  177.9 466.6 %while.2 = (u32[]{:T(128)}, f32[1,3,2096128]{2,1,0:T(4,128)}, f32[6288384]{0:T(1024)}, u32[]{}, f32[]{:T(128)}, /*index=5*/u32[]{}, u32[]{}, u32[]{}) while((u32[]{:T(128)}, f32[1,3,2096128]{2,1,0:T(4,128)}, f32[6288384]{0:T(1024)}, u32[]{}, f32[]{:T(128)}, /*index=5*/u32[]{}, u32[]{}, u32[]{}) %tuple.56), condition=%wide.cond, body=%wide.body.sunk | while | flops 9 | bytes 33538248
  178.4 83.7 %dynamic-slice_reduce_fusion.5 = f32[2096128]{0:T(1024)} fusion(f32[]{:T(128)} %broadcast.345, f32[1,3,2096128]{2,1,0:T(4,128)} %get-tuple-element.128, u32[]{:T(128)S(6)} %multiply.93, u32[]{:T(128)S(6)} %multiply.94), kind=kLoop, calls=%fused_computation.208.clone.1 | loop fusion | bytes 16769036
  262.1 71.3 %dynamic-update-slice.16 = f32[6288384]{0:T(1024)} dynamic-update-slice(f32[6288384]{0:T(1024)} %get-tuple-element.121, f32[2096128]{0:T(1024)} %dynamic-slice_reduce_fusion.5, u32[]{:T(128)S(6)} %add.310) | dynamic-update-slice | bytes 16769028
  333.9 83.7 %dynamic-slice_reduce_fusion.5 = f32[2096128]{0:T(1024)} fusion(f32[]{:T(128)} %broadcast.345, f32[1,3,2096128]{2,1,0:T(4,128)} %get-tuple-element.128, u32[]{:T(128)S(6)} %multiply.93, u32[]{:T(128)S(6)} %multiply.94), kind=kLoop, calls=%fused_computation.208.clone.1 | loop fusion | bytes 16769036
  417.7 71.3 %dynamic-update-slice.16 = f32[6288384]{0:T(1024)} dynamic-update-slice(f32[6288384]{0:T(1024)} %get-tuple-element.121, f32[2096128]{0:T(1024)} %dynamic-slice_reduce_fusion.5, u32[]{:T(128)S(6)} %add.310) | dynamic-update-slice | bytes 16769028
  489.5 83.7 %dynamic-slice_reduce_fusion.5 = f32[2096128]{0:T(1024)} fusion(f32[]{:T(128)} %broadcast.345, f32[1,3,2096128]{2,1,0:T(4,128)} %get-tuple-element.128, u32[]{:T(128)S(6)} %multiply.93, u32[]{:T(128)S(6)} %multiply.94), kind=kLoop, calls=%fused_computation.208.clone.1 | loop fusion | bytes 16769036
  573.2 71.3 %dynamic-update-slice.16 = f32[6288384]{0:T(1024)} dynamic-update-slice(f32[6288384]{0:T(1024)} %get-tuple-element.121, f32[2096128]{0:T(1024)} %dynamic-slice_reduce_fusion.5, u32[]{:T(128)S(6)} %add.310) | dynamic-update-slice | bytes 16769028
  644.5 37.4 %reshape.526 = f32[3,1024,2047]{2,1,0:T(8,128)} reshape(f32[6288384]{0:T(1024)} %get-tuple-element.14) | data formatting | bytes 50307072 | tf_op jit(solution)/shard_map/reshape | solution.py:101
  776.7 49.1 %all-gather.25.cloned.1.call-done = bf16[768,1536]{1,0:T(8,128)(2,1)} async-done(((bf16[96,1536]{1,0:T(8,128)(2,1)}), bf16[768,1536]{1,0:T(8,128)(2,1)}) %all-gather.25.cloned.1.call-update) | async-done | bytes 2359312 | tf_op jit(solution)/shard_map/all_gather | solution.py:73
  853.5 37.2 %all-gather.33.cloned.1.call-done = bf16[1,768,768]{2,1,0:T(8,128)(2,1)} async-done(((bf16[1,96,768]{2,1,0:T(8,128)(2,1)}), bf16[1,768,768]{2,1,0:T(8,128)(2,1)}) %all-gather.33.cloned.1.call-update) | async-done | bytes 1179664 | tf_op jit(solution)/shard_map/all_gather | solution.py:73
  1015.6 40.4 %reduce-scatter.20.cloned.1.call-done = bf16[96,768]{1,0:T(8,128)(2,1)} async-done(((bf16[768,768]{1,0:T(8,128)(2,1)}), bf16[96,768]{1,0:T(8,128)(2,1)}) %reduce-scatter.20.cloned.1.call-update) | async-done | bytes 147472 | tf_op jit(solution)/shard_map/reduce_scatter | solution.py:76
  1064.8 63.5 %reduce-scatter.18.cloned.1.call-done = bf16[96,1536]{1,0:T(8,128)(2,1)} async-done(((bf16[768,1536]{1,0:T(8,128)(2,1)}), bf16[96,1536]{1,0:T(8,128)(2,1)}) %reduce-scatter.18.cloned.1.call-update) | async-done | bytes 294928 | tf_op jit(solution)/shard_map/reduce_scatter | solution.py:76
  1156.2 96.0 %rev.3 = f32[3,1024,1024]{1,2,0:T(8,128)} reverse(f32[3,1024,1024]{1,2,0:T(8,128)} %get-tuple-element.50), dimensions={2} | reverse | bytes 25165824 | tf_op jit(solution)/shard_map/rev | solution.py:171
  1279.2 33.4 %copy.148 = f32[1,3,1024,2048]{3,1,2,0:T(4,128)} copy(f32[1,3,1024,2048]{3,2,1,0:T(8,128)} %pad_bitcast_fusion) | data formatting | bytes 50331648
  1360.1 466.7 %while.3 = (u32[]{:T(128)}, f32[1,3,2096128]{2,1,0:T(4,128)}, f32[6288384]{0:T(1024)}, u32[]{}, f32[]{:T(128)}, /*index=5*/u32[]{}, u32[]{}, u32[]{}) while((u32[]{:T(128)}, f32[1,3,2096128]{2,1,0:T(4,128)}, f32[6288384]{0:T(1024)}, u32[]{}, f32[]{:T(128)}, /*index=5*/u32[]{}, u32[]{}, u32[]{}) %tuple.59), condition=%wide.cond.1, body=%wide.body.1.sunk | while | flops 9 | bytes 33538248
  1360.6 83.8 %dynamic-slice_reduce_fusion.6 = f32[2096128]{0:T(1024)} fusion(f32[]{:T(128)} %broadcast.346, f32[1,3,2096128]{2,1,0:T(4,128)} %get-tuple-element.152, u32[]{:T(128)S(6)} %multiply.97, u32[]{:T(128)S(6)} %multiply.98), kind=kLoop, calls=%fused_computation.209.clone.1 | loop fusion | bytes 16769036
  1444.4 71.3 %dynamic-update-slice.17 = f32[6288384]{0:T(1024)} dynamic-update-slice(f32[6288384]{0:T(1024)} %get-tuple-element.145, f32[2096128]{0:T(1024)} %dynamic-slice_reduce_fusion.6, u32[]{:T(128)S(6)} %add.312) | dynamic-update-slice | bytes 16769028
  1516.2 83.7 %dynamic-slice_reduce_fusion.6 = f32[2096128]{0:T(1024)} fusion(f32[]{:T(128)} %broadcast.346, f32[1,3,2096128]{2,1,0:T(4,128)} %get-tuple-element.152, u32[]{:T(128)S(6)} %multiply.97, u32[]{:T(128)S(6)} %multiply.98), kind=kLoop, calls=%fused_computation.209.clone.1 | loop fusion | bytes 16769036
  1599.9 71.3 %dynamic-update-slice.17 = f32[6288384]{0:T(1024)} dynamic-update-slice(f32[6288384]{0:T(1024)} %get-tuple-element.145, f32[2096128]{0:T(1024)} %dynamic-slice_reduce_fusion.6, u32[]{:T(128)S(6)} %add.312) | dynamic-update-slice | bytes 16769028
  1671.8 83.7 %dynamic-slice_reduce_fusion.6 = f32[2096128]{0:T(1024)} fusion(f32[]{:T(128)} %broadcast.346, f32[1,3,2096128]{2,1,0:T(4,128)} %get-tuple-element.152, u32[]{:T(128)S(6)} %multiply.97, u32[]{:T(128)S(6)} %multiply.98), kind=kLoop, calls=%fused_computation.209.clone.1 | loop fusion | bytes 16769036
  1755.5 71.3 %dynamic-update-slice.17 = f32[6288384]{0:T(1024)} dynamic-update-slice(f32[6288384]{0:T(1024)} %get-tuple-element.145, f32[2096128]{0:T(1024)} %dynamic-slice_reduce_fusion.6, u32[]{:T(128)S(6)} %add.312) | dynamic-update-slice | bytes 16769028
  1832.2 37.1 %reshape.540 = f32[3,1024,2047]{2,1,0:T(8,128)} reshape(f32[6288384]{0:T(1024)} %get-tuple-element.19) | data formatting | bytes 50307072 | tf_op jit(solution)/shard_map/reshape | solution.py:172
  1879.2 39.4 %psum.15 = f32[66,12]{0,1:T(8,128)S(1)} all-reduce(f32[66,12]{0,1:T(8,128)S(1)} %dynamic_update_slice.3), channel_id=1, replica_groups=mesh['dp'=8,'seq'=4] {'dp','seq'}, use_global_device_ids=true, to_apply=%region_32.33 | all-reduce | flops 792 | bytes 6336 | tf_op jit(solution)/shard_map/psum | solution.py:179
  (277 shorter events, 595.4 us)
Async XLA Ops:
  8.0 767.1 %copy-start = (bf16[384,768]{1,0:T(8,128)(2,1)S(1)}, bf16[384,768]{1,0:T(8,128)(2,1)}, u32[]{:S(2)}) copy-start(bf16[384,768]{1,0:T(8,128)(2,1)} %param.18) | copy-start | bytes 1769476
  8.0 58.7 %copy-start.39 = (bf16[256]{0:T(256)(128)(2,1)S(1)}, bf16[256]{0:T(256)(128)(2,1)}, u32[]{:S(2)}) copy-start(bf16[256]{0:T(256)(128)(2,1)} %param.21) | copy-start | bytes 1540
  8.0 58.8 %copy-start.12 = (bf16[66,256]{1,0:T(8,128)(2,1)S(1)}, bf16[66,256]{1,0:T(8,128)(2,1)}, u32[]{:S(2)}) copy-start(bf16[66,256]{1,0:T(8,128)(2,1)} %param.20) | copy-start | bytes 101380
  8.0 59.1 %copy-start.29 = (bf16[256,12]{0,1:T(8,128)(2,1)S(1)}, bf16[256,12]{0,1:T(8,128)(2,1)}, u32[]{:S(2)}) copy-start(bf16[256,12]{0,1:T(8,128)(2,1)} %param.22) | copy-start | bytes 18436
  8.1 59.8 %copy-start.14 = (bf16[96,2304]{1,0:T(8,128)(2,1)S(1)}, bf16[96,2304]{1,0:T(8,128)(2,1)}, u32[]{:S(2)}) copy-start(bf16[96,2304]{1,0:T(8,128)(2,1)} %param.15) | copy-start | bytes 1327108
  8.1 701.0 %all-reduce.4.cloned.1.call-start = ((), (), s32[]{:S(2)}) async-start(), calls=%async_computation.23 | async-start | bytes 294912
  32.6 678.1 %all-gather.19.cloned.1.call-start = ((), (), s32[]{:S(2)}) async-start(), calls=%async_computation.7 | async-start | bytes 1966080 | tf_op jit(solution)/shard_map/all_gather | solution.py:73
  33.2 730.8 %all-gather.31.cloned.1.call-start = ((), (), s32[]{:S(2)}) async-start(), calls=%async_computation.19 | async-start | bytes 1474560 | tf_op jit(solution)/shard_map/all_gather | solution.py:73
  66.7 704.4 %all-gather.21.cloned.1.call-start = ((), (), s32[]{:S(2)}) async-start(), calls=%async_computation.8 | async-start | bytes 1966080 | tf_op jit(solution)/shard_map/all_gather | solution.py:73
  754.2 71.6 %all-gather.25.cloned.1.call-start = ((), (), s32[]{:S(2)}) async-start(), calls=%async_computation.10 | async-start | bytes 2654208 | tf_op jit(solution)/shard_map/all_gather | solution.py:73
  763.9 82.2 %all-gather.23.cloned.1.call-start = ((), (), s32[]{:S(2)}) async-start(), calls=%async_computation.9 | async-start | bytes 1966080 | tf_op jit(solution)/shard_map/all_gather | solution.py:73
  775.1 115.6 %all-gather.33.cloned.1.call-start = ((), (), s32[]{:S(2)}) async-start(), calls=%async_computation.20 | async-start | bytes 1327104 | tf_op jit(solution)/shard_map/all_gather | solution.py:73
  775.8 134.4 %all-gather.27.cloned.1.call-start = ((), (), s32[]{:S(2)}) async-start(), calls=%async_computation.12 | async-start | bytes 1966080 | tf_op jit(solution)/shard_map/all_gather | solution.py:73
  776.4 174.8 %reduce-scatter.12.cloned.1.call-start = ((), (), s32[]{:S(2)}) async-start(), calls=%async_computation.13 | async-start | bytes 1966080 | tf_op jit(solution)/shard_map/reduce_scatter | solution.py:76
  923.0 58.8 %reduce-scatter.10.cloned.1.call-start = ((), (), s32[]{:S(2)}) async-start(), calls=%async_computation.11 | async-start | bytes 1966080 | tf_op jit(solution)/shard_map/reduce_scatter | solution.py:76
  923.1 58.7 %copy-start.9 = (bf16[1,256,768]{2,1,0:T(8,128)(2,1)S(1)}, bf16[1,256,768]{2,1,0:T(8,128)(2,1)}, u32[]{:S(2)}) copy-start(bf16[1,256,768]{2,1,0:T(8,128)(2,1)} %param.25) | copy-start | bytes 1179652
  927.5 78.9 %all-gather.29.cloned.1.call-start = ((), (), s32[]{:S(2)}) async-start(), calls=%async_computation.14 | async-start | bytes 1966080 | tf_op jit(solution)/shard_map/all_gather | solution.py:73
  986.8 69.2 %reduce-scatter.20.cloned.1.call-start = ((), (), s32[]{:S(2)}) async-start(), calls=%async_computation.18 | async-start | bytes 1327104 | tf_op jit(solution)/shard_map/reduce_scatter | solution.py:76
  991.2 137.2 %reduce-scatter.18.cloned.1.call-start = ((), (), s32[]{:S(2)}) async-start(), calls=%async_computation.17 | async-start | bytes 2654208 | tf_op jit(solution)/shard_map/reduce_scatter | solution.py:76
  997.8 923.5 %reduce-scatter.16.cloned.1.call-start = ((), (), s32[]{:S(2)}) async-start(), calls=%async_computation.16 | async-start | bytes 442368 | tf_op jit(solution)/shard_map/reduce_scatter | solution.py:76
  1009.5 919.5 %all-gather.35.cloned.1.call-start = ((), (), s32[]{:S(2)}) async-start(), calls=%async_computation.21 | async-start | bytes 1474560 | tf_op jit(solution)/shard_map/all_gather | solution.py:200
  1015.6 114.9 %copy-start.16 = (bf16[1,1024,192]{1,2,0:T(8,128)(2,1)S(1)}, bf16[1,1024,192]{1,2,0:T(8,128)(2,1)}, u32[]{:S(2)}) copy-start(bf16[1,1024,192]{1,2,0:T(8,128)(2,1)} %copy-done.15) | copy-start | bytes 1179652
  1128.4 815.2 %reduce-scatter.22.cloned.1.call-start = ((), (), s32[]{:S(2)}) async-start(), calls=%async_computation.22 | async-start | bytes 1105920 | tf_op jit(solution)/shard_map/reduce_scatter | solution.py:76
  1334.7 622.4 %reduce-scatter.14.cloned.1.call-start = ((), (), s32[]{:S(2)}) async-start(), calls=%async_computation.15 | async-start | bytes 1966080 | tf_op jit(solution)/shard_map/reduce_scatter | solution.py:76
  (41 other events, 729.4 us)
Sparse Core Ops, SparseCore 0:
  32.8 67.7 all-reduce.3
  991.9 64.0 reduce-scatter.19
  1060.5 67.8 reduce-scatter.17
  1132.4 60.4 reduce-scatter.15
  1334.8 62.2 reduce-scatter.21
  1399.5 27.1 reduce-scatter.13
Sparse Core Ops, SparseCore 1:
  34.7 16.8 all-gather.18
  66.8 14.4 all-gather.30
  754.3 16.7 all-gather.20
  774.1 51.7 all-gather.24
  828.1 18.0 all-gather.22
  849.2 41.5 all-gather.32
  892.2 18.0 all-gather.26
  923.1 28.1 reduce-scatter.11
  953.7 28.1 reduce-scatter.9
  986.8 19.5 all-gather.28
  1128.4 16.3 all-gather.34

commit v2 on v1

--- a/solution.py
+++ b/solution.py
@@ -1,6 +1,11 @@
+import functools
+import types
+
 import jax
 import jax.numpy as jnp
 from jax import lax
+from jax.experimental import pallas as pl
+from jax.experimental.pallas import tpu as pltpu
 from jax.sharding import PartitionSpec as P
 
 H = 12
@@ -11,6 +16,9 @@
 HIGHEST = lax.Precision.HIGHEST
 F32 = jnp.float32
 BF16 = jnp.bfloat16
+
+
+VMEM_LIMIT = 65400 * 2**10
 
 
 def layer_norm(values):
@@ -39,7 +47,7 @@
     return jnp.einsum(spec, a, b, preferred_element_type=F32)
 
 
-def body(
+def plain_body(
     hidden_in,
     condition,
     qkv_weight,
@@ -217,6 +225,1118 @@
     )
 
 
+MESH = pl.DeviceIdType.MESH
+LANES = 128
+
+
+def nn(a, b):
+    return jnp.dot(a, b, preferred_element_type=F32)
+
+
+def nt(a, b):
+    return lax.dot_general(a, b, (((1,), (1,)), ((), ())), preferred_element_type=F32)
+
+
+def tn(a, b):
+    return lax.dot_general(a, b, (((0,), (0,)), ((), ())), preferred_element_type=F32)
+
+
+def skew(tile, back):
+    row = lax.broadcasted_iota(jnp.int32, tile.shape, 0)
+    for bit in range(7):
+        turn = LANES - (1 << bit) if back else 1 << bit
+        tile = jnp.where(((row >> bit) & 1) == 1, pltpu.roll(tile, turn, 1), tile)
+    return tile
+
+
+class Sizes:
+    def __init__(self, rows, width, seq, dp, shard, down_shard, ada_rows, conditioning):
+        self.rows, self.width, self.seq, self.dp = rows, width, seq, dp
+        self.shard, self.ada_rows, self.conditioning = shard, ada_rows, conditioning
+        self.strip = down_shard // seq
+        self.length = rows * seq
+        self.heads = H // seq
+        self.part = self.heads * DH
+        self.hidden = self.strip * dp
+        self.far = dp // 2
+        self.half = shard // 2
+        self.blocks = self.length // LANES
+
+
+class Wires:
+    def __init__(self, send, recv):
+        self.send, self.recv, self.count, self.started = send, recv, 0, []
+
+    def reserve(self, count=1):
+        first = self.count
+        self.count += count
+        return first
+
+    def make(self, number, source, target, device):
+        return pltpu.make_async_remote_copy(
+            src_ref=source,
+            dst_ref=target,
+            send_sem=self.send.at[number],
+            recv_sem=self.recv.at[number],
+            device_id=device,
+            device_id_type=MESH,
+        )
+
+    def go(self, number, source, target, device):
+        copy = self.make(number, source, target, device)
+        copy.start()
+        self.started.append(copy)
+        return copy
+
+    def settle(self, copy):
+        copy.wait_send()
+        self.started = [other for other in self.started if other is not copy]
+
+    def finish(self):
+        for copy in self.started:
+            copy.wait_send()
+        self.started = []
+
+
+def layer_kernel(sizes, names, *refs):
+    r = types.SimpleNamespace(**dict(zip(names, refs, strict=True)))
+    n = sizes
+    rows, width, part, heads, length, hid = n.rows, n.width, n.part, n.heads, n.length, n.hidden
+    half_rows = rows // 2
+    d, s = lax.axis_index("dp"), lax.axis_index("seq")
+    z, x = d // 2, lax.rem(d, 2)
+    y, c = s // 2, lax.rem(s, 2)
+    ox, oy, oc = 1 - x, 1 - y, 1 - c
+    at_x = (z * 2 + ox, s)
+    at_y = (d, oy * 2 + c)
+    at_c = (d, y * 2 + oc)
+
+    def z_plus(k):
+        return lax.rem(z + k, n.far)
+
+    def at_z(k):
+        return (z_plus(k) * 2 + x, s)
+
+    wires = Wires(r.send_sem, r.recv_sem)
+    dp_peers = [(k, e) for k in range(n.far) for e in range(2) if k or e]
+    seq_peers = [(1, 0), (0, 1), (1, 1)]
+
+    def dp_peer(k, e):
+        xx = lax.rem(x + e, 2)
+        return z_plus(k) * 2 + xx, lax.rem(z + n.far - k, n.far) * 2 + xx
+
+    def seq_peer(a, b):
+        return lax.rem(y + a, 2) * 2 + lax.rem(c + b, 2)
+
+    barrier = pltpu.get_barrier_semaphore()
+    for k, e in dp_peers:
+        pl.semaphore_signal(barrier, inc=1, device_id=(dp_peer(k, e)[0], s), device_id_type=MESH)
+    for a, b in seq_peers:
+        pl.semaphore_signal(barrier, inc=1, device_id=(d, seq_peer(a, b)), device_id_type=MESH)
+    pl.semaphore_wait(barrier, len(dp_peers) + len(seq_peers))
+
+    local_count = [0]
+
+    def local(source, target):
+        copy = pltpu.make_async_copy(source, target, r.local_sem.at[local_count[0]])
+        local_count[0] += 1
+        copy.start()
+        return copy
+
+    class SeqGather:
+        def __init__(self, block):
+            self.block, self.first = block, wires.reserve(3)
+            self.mine, self.from_y, self.from_c, self.from_yc = s, at_y[1], at_c[1], oy * 2 + oc
+
+        def start(self, source=None):
+            mine = self.block(self.mine)
+            source = mine if source is None else source
+            self.sent = [wires.go(self.first, source, mine, at_y), wires.go(self.first + 1, source, mine, at_c)]
+
+        def hand_on(self):
+            place = self.block(self.from_y)
+            wires.make(self.first, place, place, at_y).wait_recv()
+            self.sent.append(wires.go(self.first + 2, place, place, at_c))
+
+        def settle(self):
+            for copy in self.sent:
+                wires.settle(copy)
+
+        def wait_core(self):
+            place = self.block(self.from_c)
+            wires.make(self.first + 1, place, place, at_c).wait_recv()
+
+        def wait_last(self):
+            place = self.block(self.from_yc)
+            wires.make(self.first + 2, place, place, at_c).wait_recv()
+
+        def wait(self):
+            self.hand_on()
+            self.wait_core()
+            self.wait_last()
+
+    class DpGather:
+        def __init__(self, source, place):
+            self.source, self.place, self.first = source, place, wires.reserve(2 * n.far - 1)
+
+        def start(self):
+            mine = self.place(d)
+            self.own = local(self.source, mine)
+            for k in range(1, n.far):
+                wires.go(self.first + k - 1, self.source, mine, at_z(k))
+            wires.go(self.first + n.far - 1, self.source, mine, at_x)
+
+        def hand_on(self):
+            for k in range(1, n.far):
+                place = self.place(dp_peer(k, 0)[1])
+                wires.make(self.first + k - 1, place, place, at_z(k)).wait_recv()
+                wires.go(self.first + n.far - 1 + k, place, place, at_x)
+
+        def wait(self):
+            self.own.wait()
+            for k in range(n.far):
+                place = self.place(dp_peer(k, 1)[1])
+                wires.make(self.first + n.far - 1 + k, place, place, at_x).wait_recv()
+
+    class SeqReduce:
+        def __init__(self, sib, got, over, come):
+            self.sib, self.got, self.over, self.come = sib, got, over, come
+            self.first, self.sent = wires.reserve(3), []
+
+        def put_core(self, index):
+            def put(lanes, block):
+                self.sib[index, :, lanes] = block.astype(BF16)
+
+            return put
+
+        def to_core(self, index):
+            self.sent.append(wires.go(self.first + index, self.sib.at[index], self.got.at[index], at_c))
+
+        def wait_far(self):
+            wires.make(self.first + 1, self.sib.at[1], self.got.at[1], at_c).wait_recv()
+
+        def put_y(self):
+            def put(lanes, block):
+                self.over[:, lanes] = (block + self.got[1, :, lanes].astype(F32)).astype(BF16)
+
+            return put
+
+        def to_y(self):
+            self.sent.append(wires.go(self.first + 2, self.over, self.come, at_y))
+
+        def settle(self):
+            for copy in self.sent:
+                wires.settle(copy)
+
+        def wait(self):
+            wires.make(self.first, self.sib.at[0], self.got.at[0], at_c).wait_recv()
+            wires.make(self.first + 2, self.over, self.come, at_y).wait_recv()
+
+        def total(self, own, place):
+            return own[place, :] + self.got[0, place, :].astype(F32) + self.come[place, :].astype(F32)
+
+    class DpReduce:
+        def __init__(self, grad, got, come, mine, share):
+            self.grad, self.got, self.come, self.mine, self.share = grad, got, come, mine, share
+            self.first, self.second = wires.reserve(n.far), wires.reserve(n.far)
+            self.gather = SeqGather(lambda t: self.share.at[t])
+
+        def start(self):
+            for k in (*range(1, n.far), 0):
+                to = z_plus(k)
+                wires.go(self.first + k, self.grad.at[ox, to], self.got.at[to], at_x)
+
+        def along_z(self, k):
+            to = z_plus(k)
+            wires.make(self.first + k, self.grad.at[ox, to], self.got.at[to], at_x).wait_recv()
+            self.grad[x, to] = (self.grad[x, to].astype(F32) + self.got[to].astype(F32)).astype(BF16)
+            if k:
+                wires.go(self.second + k, self.grad.at[x, to], self.come.at[k - 1], at_z(k))
+
+        def finish(self):
+            total = self.grad[x, z].astype(F32)
+            for k in range(1, n.far):
+                wires.make(self.second + k, self.grad.at[x, z], self.come.at[k - 1], at_z(k)).wait_recv()
+                total = total + self.come[k - 1].astype(F32)
+            self.mine[...] = total.astype(BF16)
+            self.own = local(self.mine, self.share.at[s])
+            self.gather.start(self.mine)
+
+        def hand_on(self):
+            self.gather.hand_on()
+
+        def wait(self):
+            self.gather.wait_core()
+            self.gather.wait_last()
+            self.own.wait()
+
+    step = 32
+
+    def by_rows(count, work, start=0, unroll=2):
+        def one(q, carry):
+            return work(pl.ds(pl.multiple_of(q * step, step), step), carry)
+
+        return lax.fori_loop(0, count // step, one, start, unroll=unroll)
+
+    wide = 2 * LANES
+
+    def by_lanes(count, work):
+        def one(q, _):
+            work(pl.ds(pl.multiple_of(q * wide, wide), wide))
+            return 0
+
+        lax.fori_loop(0, count // wide, one, 0)
+
+    def fold_rows(array):
+        return jnp.sum(array.reshape(step // 8, 8, width), axis=0)
+
+    hidden_all, grads_all = r.hidden_all, r.grads_all
+
+    def rows_of(ref):
+        return lambda t: ref.at[pl.ds(pl.multiple_of(t * rows, rows), rows)]
+
+    hidden_gather, up_gather = SeqGather(rows_of(hidden_all)), SeqGather(rows_of(grads_all))
+    qkv_gather = DpGather(
+        r.qkv, lambda t: r.w_qkv.at[pl.ds(pl.multiple_of(t * n.shard, n.shard), n.shard)]
+    )
+    pieces = [
+        DpGather(
+            r.gate_up.at[:, pl.ds(q * (hid // 2), hid // 2)],
+            lambda t, q=q: r.w_gate_up.at[
+                pl.ds(pl.multiple_of(t * n.shard, n.shard), n.shard), pl.ds(q * (hid // 2), hid // 2)
+            ],
+        )
+        for q in range(4)
+    ]
+    pieces.append(
+        DpGather(r.down, lambda t: r.w_down.at[pl.ds(pl.multiple_of(t * n.strip, n.strip), n.strip)])
+    )
+    lanes_y = pl.ds(pl.multiple_of(y * (width // 2), width // 2), width // 2)
+    out_gather = DpGather(r.out, lambda t: r.w_out.at[t, c, :, lanes_y])
+    pieces.insert(2, out_gather)
+
+    def out_block(t):
+        ty, tc = t // 2, lax.rem(t, 2)
+        return r.w_out.at[:, tc, :, pl.ds(pl.multiple_of(ty * (width // 2), width // 2), width // 2)]
+
+    out_share = SeqGather(out_block)
+
+    cond_first, mod_first = wires.reserve(len(dp_peers)), wires.reserve(len(dp_peers))
+    cond_all, mod_send, mod_recv = r.cond_all, r.mod_send, r.mod_recv
+    own_cond = local(r.condition, cond_all.at[d])
+    for i, (k, e) in enumerate(dp_peers):
+        wires.go(cond_first + i, r.condition, cond_all.at[d], (dp_peer(k, e)[0], s))
+    own_hidden = local(r.hidden, hidden_gather.block(s))
+    keep_hidden = local(r.hidden, r.hidden_own)
+    keep_grads = local(r.out_grad, r.upstream)
+    hidden_gather.start(r.hidden)
+    qkv_gather.start()
+    own_grads = local(r.out_grad, up_gather.block(s))
+
+    own_cond.wait()
+    for i, (k, e) in enumerate(dp_peers):
+        place = cond_all.at[dp_peer(k, e)[1]]
+        wires.make(cond_first + i, place, place, (dp_peer(k, e)[0], s)).wait_recv()
+    item_of = lax.broadcasted_iota(jnp.int32, (n.dp, n.conditioning), 0)
+    conditions = jnp.where(item_of == 0, cond_all[0], 0.0)
+    for i in range(1, n.dp):
+        conditions = jnp.where(item_of == i, cond_all[i], conditions)
+    squashed = (conditions * (1.0 / (1.0 + jnp.exp(-conditions)))).astype(BF16).astype(F32)
+    r.squashed[...] = squashed.T
+    squashed_rows = r.squashed[pl.ds(pl.multiple_of(d * n.ada_rows, n.ada_rows), n.ada_rows), :]
+    ada_part = tn(squashed_rows.astype(BF16), r.ada[...])
+    for i in range(n.dp):
+        mod_send[i] = ada_part[i : i + 1]
+    mod_recv[d] = mod_send[d]
+    for i, (k, e) in enumerate(dp_peers):
+        wires.go(mod_first + i, mod_send.at[dp_peer(k, e)[0]], mod_recv.at[d], (dp_peer(k, e)[0], s))
+    pieces[0].start()
+    hidden_gather.hand_on()
+    up_gather.start(r.out_grad)
+    qkv_gather.hand_on()
+    pieces[1].start()
+
+    bias, lines = r.bias, r.lines
+    key_in = lax.broadcasted_iota(jnp.int32, (LANES, LANES), 0)
+    query_in = lax.broadcasted_iota(jnp.int32, (LANES, LANES), 1)
+    middle_tile = n.blocks - 1
+
+    def build_bias(h, _):
+        line = lines[h]
+        near = skew(jnp.broadcast_to(line[:, :LANES], (LANES, LANES)), False)
+        low_end = jnp.broadcast_to(line[:, LANES : LANES + 1], (LANES, LANES))
+        high_end = jnp.broadcast_to(line[:, LANES + 1 : LANES + 2], (LANES, LANES))
+        for tile in range(2 * n.blocks - 1):
+            away = tile - middle_tile
+            apart = query_in - key_in - away * LANES
+            if away < -1:
+                value = high_end
+            elif away > 1:
+                value = low_end
+            else:
+                value = jnp.where(apart >= RR, high_end, jnp.where(apart <= -RR, low_end, near))
+            bias[h, tile * LANES : (tile + 1) * LANES] = value
+        return 0
+
+    lax.fori_loop(0, heads, build_bias, 0)
+
+    own_hidden.wait()
+    hidden_gather.wait_core()
+    hidden_gather.wait_last()
+    for i, (k, e) in enumerate(dp_peers):
+        place = mod_recv.at[dp_peer(k, e)[1]]
+        wires.make(mod_first + i, mod_send.at[d], place, (dp_peer(k, e)[0], s)).wait_recv()
+    modulation = mod_recv[0]
+    for i in range(1, n.dp):
+        modulation = modulation + mod_recv[i]
+    r.modulation[...] = modulation
+
+    def vector(index):
+        return r.modulation[:, index * width : (index + 1) * width]
+
+    shift_one, scale_one, gate_one, shift_two, scale_two, gate_two = range(6)
+    first = hidden_all
+    hidden_gather.settle()
+
+    def make_first(place, _):
+        normal, _ = layer_norm(hidden_all[place, :].astype(F32))
+        first[place, :] = (normal * (1.0 + vector(scale_one)) + vector(shift_one)).astype(BF16)
+        return 0
+
+    by_rows(length, make_first)
+
+    qkv_gather.wait()
+    w_qkv = r.w_qkv
+    keys, values, queries = r.keys, r.values, r.queries
+    keys_t, values_t, queries_t = r.keys_t, r.values_t, r.queries_t
+    w_qkv_t = r.inner_t
+
+    def turn_weight(q, _):
+        place = pl.ds(pl.multiple_of(q * 2 * LANES, 2 * LANES), 2 * LANES)
+        w_qkv_t[0 : 3 * part, place] = w_qkv[place, :].T
+        return 0
+
+    lax.fori_loop(0, width // (2 * LANES), turn_weight, 0)
+
+    def project(t, _):
+        place = pl.ds(pl.multiple_of(t * rows, rows), rows)
+        block = first[place, :]
+        for low in range(0, 3 * part, wide):
+            merged = nn(block, w_qkv[:, low : min(low + wide, 3 * part)]).astype(BF16)
+            for q in range(merged.shape[1] // DH):
+                kind, h = divmod(low // DH + q, heads)
+                column = merged[:, q * DH : (q + 1) * DH]
+                if kind == 0:
+                    column = (column.astype(F32) * 0.125).astype(BF16)
+                (queries, keys, values)[kind][h, place, :] = column
+        for kind, target in enumerate((queries_t, keys_t, values_t)):
+            merged_t = nt(w_qkv_t[kind * part : (kind + 1) * part, 0:width], block).astype(BF16)
+            if kind == 0:
+                merged_t = (merged_t.astype(F32) * 0.125).astype(BF16)
+            for h in range(heads):
+                target[h, t] = merged_t[h * DH : (h + 1) * DH]
+        return 0
+
+    lax.fori_loop(0, n.seq, project, 0)
+
+    valid, broken = r.valid_len[0], r.chain_break[0]
+    exps, outs_t, inverse = r.exps, r.outs_t, r.inverse
+    tiles = rows // LANES
+    order = [oy * 2 + c, oy * 2 + oc, y * 2 + oc, s]
+
+    raw = r.raw
+
+    def tile_parts(t, tile):
+        number = t * tiles + tile
+        query_side = number * LANES + lax.broadcasted_iota(jnp.int32, (1, LANES), 1) >= broken
+        for q in range(n.blocks):
+            key_pos = q * LANES + lax.broadcasted_iota(jnp.int32, (LANES, LANES), 0)
+            strip = pl.ds(pl.multiple_of((n.blocks - 1 + q - number) * LANES, LANES), LANES)
+            yield slice(q * LANES, (q + 1) * LANES), strip, key_pos, (key_pos >= broken) == query_side
+
+    def eights(array):
+        return array.reshape(LANES // 8, 8, LANES)
+
+    def attend(t):
+        def one_head(h, _):
+            for q in range(n.seq):
+                place = slice(q * rows, (q + 1) * rows)
+                raw[place, :] = nn(keys[h, place, :], queries_t[h, t])
+            for tile in range(tiles):
+                lanes = slice(tile * LANES, (tile + 1) * LANES)
+                far_side = jnp.broadcast_to(lines[h][:, LANES + 2 : LANES + 3], (1, LANES))
+                top = jnp.full((8, LANES), -1e30, F32)
+                for place, strip, key_pos, same in tile_parts(t, tile):
+                    logits = raw[place, lanes] + jnp.where(same, bias[h, strip, :], far_side)
+                    logits = jnp.where(key_pos < valid, logits, -1e30)
+                    raw[place, lanes] = logits
+                    top = jnp.maximum(top, jnp.max(eights(logits), axis=0))
+                top = jnp.max(top, axis=0, keepdims=True)
+                total = jnp.zeros((8, LANES), F32)
+                for q in range(n.blocks):
+                    place = slice(q * LANES, (q + 1) * LANES)
+                    powers = jnp.exp(raw[place, lanes] - top)
+                    total = total + jnp.sum(eights(powers), axis=0)
+                    exps[h, t, place, lanes] = powers.astype(BF16)
+                inverse[h, t, :, lanes] = 1.0 / jnp.sum(total, axis=0, keepdims=True)
+            values_wide = jnp.concatenate([values_t[h, q] for q in range(n.seq)], axis=1)
+            outs_t[h, t] = nn(values_wide, exps[h, t]) * inverse[h, t]
+            return 0
+
+        lax.fori_loop(0, heads, one_head, 0)
+
+    mixed_first = wires.reserve(3)
+    mixed_send, mixed_recv = r.mixed_send, r.mixed_recv
+    mixed_sent = []
+    to_send = [at_y, (d, oy * 2 + oc), at_c]
+    for i, t in enumerate(order):
+        attend(t)
+        block = jnp.concatenate([outs_t[h, t] for h in range(heads)], axis=0).T.astype(BF16)
+        if i < 3:
+            mixed_send[i] = block
+            mixed_sent.append(wires.go(mixed_first + i, mixed_send.at[i], mixed_recv.at[s], to_send[i]))
+        else:
+            mixed_recv[s] = block
+        pieces[i].hand_on()
+        pieces[i + 2].start()
+    up_gather.hand_on()
+
+    out_gather.wait()
+    out_share.start()
+    out_share.wait()
+
+    def w_out(q, lanes=slice(None)):
+        shards = part // n.shard
+        block = r.w_out[q * shards : (q + 1) * shards, :, :, lanes]
+        return block.reshape(part, block.shape[-1])
+
+    for i in range(3):
+        place = mixed_recv.at[order[i]]
+        wires.make(mixed_first + i, mixed_send.at[i], place, to_send[i]).wait_recv()
+    keep_hidden.wait()
+
+    def make_branch(lanes):
+        branch = nn(mixed_recv[0], w_out(0, lanes))
+        for q in range(1, n.seq):
+            branch = branch + nn(mixed_recv[q], w_out(q, lanes))
+        r.branch[:, lanes] = branch
+
+    by_lanes(width, make_branch)
+    second_all = r.second_all
+    second_gather = SeqGather(rows_of(second_all))
+
+    def make_second(place, _):
+        middle = r.hidden_own[place, :].astype(F32) + vector(gate_one) * r.branch[place, :]
+        r.middle[place, :] = middle
+        normal, _ = layer_norm(middle)
+        r.branch_grad[place, :] = (normal * (1.0 + vector(scale_two)) + vector(shift_two)).astype(BF16)
+        return 0
+
+    by_rows(rows, make_second)
+    second_all[pl.ds(pl.multiple_of(s * rows, rows), rows), :] = r.branch_grad[...]
+    second_gather.start()
+    pieces[4].hand_on()
+
+    own_grads.wait()
+    up_gather.wait_core()
+    up_gather.wait_last()
+    up_gather.settle()
+    feed_grads = grads_all
+
+    def make_feed_grads(place, _):
+        feed_grads[place, :] = (vector(gate_two) * grads_all[place, :].astype(F32)).astype(BF16)
+        return 0
+
+    by_rows(length, make_feed_grads)
+    pieces[5].hand_on()
+    for piece in pieces:
+        if piece is not out_gather:
+            piece.wait()
+    second_gather.hand_on()
+    w_gate_up, w_down = r.w_gate_up, r.w_down
+    inner, inner_t, gate_up_grads, second_t = r.inner, r.inner_t, r.gate_up_grads, r.second_t
+    feed_places = (r.feed_sib, r.feed_got, r.feed_over, r.feed_come)
+    feed_reduce = SeqReduce(*feed_places)
+    second_reduce = SeqReduce(r.second_sib, r.second_got, r.second_over, r.second_come)
+
+    def feed_forward(t, put_second, put_feed):
+        place = pl.ds(pl.multiple_of(t * rows, rows), rows)
+        lanes_t = pl.ds(pl.multiple_of(t * rows, rows), rows)
+        block = second_all[place, :]
+        second_t[:, lanes_t] = block.T
+        given = feed_grads[place, :]
+
+        def units(q, _):
+            low = pl.multiple_of(q * wide, wide)
+            gates, ups, inner_grads = raw.at[0:rows], raw.at[rows : 2 * rows], raw.at[2 * rows : 3 * rows]
+            gates[...] = nn(block, w_gate_up[:, pl.ds(low, wide)])
+            ups[...] = nn(block, w_gate_up[:, pl.ds(low + hid, wide)])
+            inner_grads[...] = nt(given, w_down[pl.ds(low, wide), :])
+            for part_of in range(rows // step):
+                few = slice(part_of * step, (part_of + 1) * step)
+                gate, up, inner_grad = gates[few, :], ups[few, :], inner_grads[few, :]
+                sigmoid = 1.0 / (1.0 + jnp.exp(-gate))
+                silu = gate * sigmoid
+                inner[few, pl.ds(low, wide)] = (silu * up).astype(BF16)
+                to = pl.ds(pl.multiple_of(t * rows + part_of * step, step), step)
+                gate_up_grads[to, pl.ds(low, wide)] = (
+                    inner_grad * up * sigmoid * (1.0 + gate * (1.0 - sigmoid))
+                ).astype(BF16)
+                gate_up_grads[to, pl.ds(low + hid, wide)] = (inner_grad * silu).astype(BF16)
+            inner_t[pl.ds(low, wide), lanes_t] = inner[:, pl.ds(low, wide)].T
+            return 0
+
+        lax.fori_loop(0, hid // wide, units, 0)
+        by_lanes(width, lambda lanes: put_second(lanes, nt(gate_up_grads[place, :], w_gate_up[lanes, :])))
+        by_lanes(width, lambda lanes: put_feed(lanes, nn(inner[...], w_down[:, lanes])))
+
+    def put_in(ref):
+        def put(lanes, block):
+            ref[:, lanes] = block.astype(ref.dtype)
+
+        return put
+
+    feed_forward(s, put_in(r.second_own), put_in(r.feed_own))
+    second_gather.wait_core()
+    feed_forward(y * 2 + oc, second_reduce.put_core(0), feed_reduce.put_core(0))
+    second_reduce.to_core(0)
+    feed_reduce.to_core(0)
+    second_gather.wait_last()
+    feed_forward(oy * 2 + oc, second_reduce.put_core(1), feed_reduce.put_core(1))
+    second_reduce.to_core(1)
+    feed_reduce.to_core(1)
+    second_reduce.wait_far()
+    feed_reduce.wait_far()
+    feed_forward(oy * 2 + c, second_reduce.put_y(), feed_reduce.put_y())
+    second_reduce.to_y()
+    feed_reduce.to_y()
+
+    gate_up_reduce = DpReduce(r.gate_up_grad, r.gate_up_got, r.gate_up_come, r.gate_up_mine, r.gate_up_share)
+    down_reduce = DpReduce(r.down_grad, r.down_got, r.down_come, r.down_mine, r.down_share)
+    out_reduce = DpReduce(r.proj_grad, r.proj_got, r.proj_come, r.proj_mine, r.proj_share)
+    qkv_reduce = DpReduce(r.qkv_grad, r.qkv_got, r.qkv_come, r.qkv_mine, r.qkv_share)
+
+    def weight_grad(left_t, right, reduce, columns, step):
+        def block(q, _):
+            low = pl.multiple_of(q * step, step)
+            height = reduce.grad.shape[2]
+            few = n.dp // 2
+            for first_of in range(0, n.dp, few):
+                grad = nn(left_t[first_of * height : (first_of + few) * height, :], right[:, pl.ds(low, step)]).astype(BF16)
+                for i in range(few):
+                    to = first_of + i
+                    reduce.grad[to % 2, to // 2, :, pl.ds(low, step)] = grad[i * height : (i + 1) * height]
+            return 0
+
+        lax.fori_loop(0, columns // step, block, 0)
+
+    weight_grad(second_t, gate_up_grads, gate_up_reduce, 2 * hid, wide)
+    gate_up_reduce.start()
+    weight_grad(inner_t, feed_grads, down_reduce, width, wide)
+    down_reduce.start()
+    lax.fori_loop(0, width // (2 * LANES), turn_weight, 0)
+
+    sums = r.mod_sums
+
+    upstream = r.upstream
+    keep_grads.wait()
+    second_reduce.wait()
+    kept_middle_grad, branch_grad = r.second_own, r.branch_grad
+    empty = jnp.zeros((8, width), F32)
+
+    def put_sum(index, array):
+        sums[s, :, index * width : (index + 1) * width] = jnp.sum(array, axis=0, keepdims=True)
+
+    def second_back(place, carry):
+        second_grad = second_reduce.total(r.second_own, place)
+        normal, inverted = layer_norm(r.middle[place, :])
+        middle_grad = upstream[place, :].astype(F32) + norm_back(
+            second_grad * (1.0 + vector(scale_two)), normal, inverted
+        )
+        kept_middle_grad[place, :] = middle_grad
+        branch_grad[place, :] = (vector(gate_one) * middle_grad).astype(BF16)
+        terms = (second_grad, second_grad * normal, middle_grad * r.branch[place, :])
+        return tuple(total + fold_rows(term) for total, term in zip(carry, terms))
+
+    for index, total in zip(
+        (shift_two, scale_two, gate_one), by_rows(rows, second_back, (empty, empty, empty))
+    ):
+        put_sum(index, total)
+    back_first = wires.reserve(3)
+    for copy in mixed_sent:
+        wires.settle(copy)
+    back_all, back_recv = mixed_send, r.back_recv
+    for q in range(n.seq):
+        back_all[q] = nt(branch_grad[...], w_out(q)).astype(BF16)
+    for i in range(3):
+        wires.go(back_first + i, back_all.at[order[i]], back_recv.at[s], to_send[i])
+    back_recv[s] = back_all[s]
+
+    out_first = wires.reserve(2)
+    second_gather.settle()
+    out_parts, quarter = second_all, n.dp * n.half
+
+    def make_out_grad(lanes):
+        for q in range(n.seq):
+            grad = tn(mixed_recv[q], branch_grad[:, lanes]).astype(BF16)
+            for i in range(part // n.half):
+                number = q * (part // n.half) + i
+                low = (number % 2) * quarter + (number // 2) * n.half
+                out_parts[low : low + n.half, lanes] = grad[i * n.half : (i + 1) * n.half]
+
+    by_lanes(width, make_out_grad)
+
+    feed_reduce.wait()
+
+    def make_result(place, total):
+        feed = feed_reduce.total(r.feed_own, place)
+        r.result[place, :] = (r.middle[place, :] + vector(gate_two) * feed).astype(BF16)
+        return total + fold_rows(upstream[place, :].astype(F32) * feed)
+
+    put_sum(gate_two, by_rows(rows, make_result, empty))
+
+    def out_rows(core):
+        return out_parts.at[pl.ds(pl.multiple_of(core * quarter, quarter), quarter)]
+
+    wires.go(out_first, out_rows(oc), r.out_near, at_c)
+    lanes_oy = pl.ds(pl.multiple_of(oy * (width // 2), width // 2), width // 2)
+
+    def out_cores():
+        wires.make(out_first, out_rows(oc), r.out_near, at_c).wait_recv()
+        mine = out_parts[pl.ds(pl.multiple_of(c * quarter, quarter), quarter), :]
+        r.out_near[...] = (r.out_near[...].astype(F32) + mine.astype(F32)).astype(BF16)
+        wires.go(out_first + 1, r.out_near.at[:, lanes_oy], r.out_far, at_y)
+
+    def out_sum():
+        wires.make(out_first + 1, r.out_near.at[:, lanes_oy], r.out_far, at_y).wait_recv()
+        total = (r.out_near[:, lanes_y].astype(F32) + r.out_far[...].astype(F32)).astype(BF16)
+        for to in range(n.dp):
+            r.proj_grad[to % 2, to // 2] = total[to * n.half : (to + 1) * n.half]
+        out_reduce.start()
+
+    dots, dots_t, delta = r.dots, r.dots_t, r.delta
+    pair_grads, query_grads = r.pair_grads, r.query_grads
+    bias[...] = jnp.zeros_like(bias)
+    pair_grads[...] = jnp.zeros_like(pair_grads)
+    crossed, score_grad = r.crossed, r.score_grad
+    crossed[...] = jnp.zeros_like(crossed)
+
+    def attend_back(t):
+        given_t = back_recv[t].T.astype(F32)
+        for h in range(heads):
+            scaled = (given_t[h * DH : (h + 1) * DH] * inverse[h, t]).astype(BF16)
+            dots_t[h] = scaled
+            dots[h] = scaled.T
+            delta[h] = jnp.sum(scaled.astype(F32) * outs_t[h, t], axis=0, keepdims=True)
+        place = pl.ds(pl.multiple_of(t * rows, rows), rows)
+
+        def one_head(h, _):
+            for q in range(n.seq):
+                some = slice(q * rows, (q + 1) * rows)
+                raw[some, :] = nn(values[h, some, :], dots_t[h])
+            for tile in range(tiles):
+                lanes = slice(tile * LANES, (tile + 1) * LANES)
+                across = jnp.zeros((8, LANES), F32)
+                for keys_of, strip, _, same in tile_parts(t, tile):
+                    grad = exps[h, t, keys_of, lanes].astype(F32) * (raw[keys_of, lanes] - delta[h, :, lanes])
+                    kept = jnp.where(same, grad, 0.0)
+                    bias[h, strip, :] = bias[h, strip, :] + kept
+                    across = across + jnp.sum(eights(grad - kept), axis=0)
+                    score_grad[keys_of, lanes] = grad.astype(BF16)
+                crossed[h] = crossed[h] + jnp.sum(across, axis=0, keepdims=True)
+            keys_wide = jnp.concatenate([keys_t[h, q] for q in range(n.seq)], axis=1)
+            query_grads[h, place, :] = (nn(keys_wide, score_grad[...]) * 0.125).T.astype(BF16)
+            for q in range(n.seq):
+                some = slice(q * rows, (q + 1) * rows)
+                pair_grads[h, some, :] = pair_grads[h, some, :] + jnp.concatenate(
+                    [nn(score_grad[some, :], queries[h, place, :]), nn(exps[h, t, some, :], dots[h])], axis=1
+                )
+            return 0
+
+        lax.fori_loop(0, heads, one_head, 0)
+
+    gate_up_reduce.along_z(1)
+    attend_back(order[3])
+    gate_up_reduce.along_z(2)
+    out_cores()
+    wires.make(back_first + 2, back_recv.at[order[2]], back_recv.at[order[2]], to_send[2]).wait_recv()
+    attend_back(order[2])
+    gate_up_reduce.along_z(3)
+    out_sum()
+    wires.make(back_first, back_recv.at[order[0]], back_recv.at[order[0]], to_send[0]).wait_recv()
+    attend_back(order[0])
+    gate_up_reduce.along_z(0)
+    down_reduce.along_z(1)
+    wires.make(back_first + 1, back_recv.at[order[1]], back_recv.at[order[1]], to_send[1]).wait_recv()
+    attend_back(order[1])
+    down_reduce.along_z(2)
+
+    feed_reduce.settle()
+    first_reduce = SeqReduce(*feed_places)
+    merged_grads = gate_up_grads
+
+    def first_part(t, put):
+        place = pl.ds(pl.multiple_of(t * rows, rows), rows)
+        merged = jnp.concatenate(
+            [query_grads[h, place, :] for h in range(heads)]
+            + [pair_grads[h, place, 0:DH].astype(BF16) for h in range(heads)]
+            + [pair_grads[h, place, DH : 2 * DH].astype(BF16) for h in range(heads)],
+            axis=1,
+        )
+        merged_grads[place, 0 : 3 * part] = merged
+        by_lanes(width, lambda lanes: put(lanes, nn(merged_grads[place, 0 : 3 * part], w_qkv_t[0 : 3 * part, lanes])))
+
+    first_part(oy * 2 + oc, first_reduce.put_core(1))
+    first_reduce.to_core(1)
+    first_part(y * 2 + oc, first_reduce.put_core(0))
+    first_reduce.to_core(0)
+    first_reduce.wait_far()
+    first_part(oy * 2 + c, first_reduce.put_y())
+    first_reduce.to_y()
+    first_part(s, put_in(r.feed_own))
+
+    def turn_first(t, _):
+        place = pl.ds(pl.multiple_of(t * rows, rows), rows)
+        second_t[:, place] = first[place, :].T
+        return 0
+
+    lax.fori_loop(0, n.seq, turn_first, 0)
+
+    def qkv_grad(q, _):
+        low = pl.multiple_of(q * 2 * n.shard, 2 * n.shard)
+        grad = nn(second_t[pl.ds(low, 2 * n.shard), :], merged_grads[:, 0 : 3 * part]).astype(BF16)
+        qkv_reduce.grad[0, q] = grad[: n.shard]
+        qkv_reduce.grad[1, q] = grad[n.shard :]
+        return 0
+
+    lax.fori_loop(0, n.far, qkv_grad, 0)
+    qkv_reduce.start()
+    for k in (3, 0):
+        down_reduce.along_z(k)
+
+    table_sums, table_all = r.table_sums, r.table_all
+
+    def fold(h, _):
+        lane = lax.broadcasted_iota(jnp.int32, (1, LANES), 1)
+        near = jnp.zeros((LANES, LANES), F32)
+        low_end = jnp.zeros((LANES, LANES), F32)
+        high_end = jnp.zeros((LANES, LANES), F32)
+        for tile in range(2 * n.blocks - 1):
+            away = tile - middle_tile
+            apart = query_in - key_in - away * LANES
+            value = bias[h, tile * LANES : (tile + 1) * LANES]
+            if away < -1:
+                high_end = high_end + value
+            elif away > 1:
+                low_end = low_end + value
+            else:
+                high_end = high_end + jnp.where(apart >= RR, value, 0.0)
+                low_end = low_end + jnp.where(apart <= -RR, value, 0.0)
+                near = near + jnp.where((apart < RR) & (apart > -RR), value, 0.0)
+        line = jnp.sum(skew(near, True), axis=0, keepdims=True)
+        for where, array in ((40, low_end), (41, high_end), (42, crossed[h])):
+            line = jnp.where(lane == where, jnp.sum(array), line)
+        table_sums[d, h] = line
+        return 0
+
+    lax.fori_loop(0, heads, fold, 0)
+    table_first = wires.reserve(len(dp_peers))
+    for i, (k, e) in enumerate(dp_peers):
+        wires.go(table_first + i, table_sums.at[d], table_sums.at[d], (dp_peer(k, e)[0], s))
+
+    first_reduce.wait()
+
+    def first_back(place, carry):
+        first_grad = first_reduce.total(r.feed_own, place)
+        normal, inverted = layer_norm(r.hidden_own[place, :].astype(F32))
+        r.input_grad[place, :] = (
+            kept_middle_grad[place, :] + norm_back(first_grad * (1.0 + vector(scale_one)), normal, inverted)
+        ).astype(BF16)
+        return tuple(total + fold_rows(term) for total, term in zip(carry, (first_grad, first_grad * normal)))
+
+    for index, total in zip((shift_one, scale_one), by_rows(rows, first_back, (empty, empty))):
+        put_sum(index, total)
+    sums_first = wires.reserve(3)
+    for i, (a, b) in enumerate(seq_peers):
+        wires.go(sums_first + i, sums.at[s], sums.at[s], (d, seq_peer(a, b)))
+    for k in (1, 2, 3, 0):
+        out_reduce.along_z(k)
+    gate_up_reduce.finish()
+    for k in (1, 2, 3, 0):
+        qkv_reduce.along_z(k)
+    down_reduce.finish()
+    out_reduce.finish()
+    for i, (k, e) in enumerate(dp_peers):
+        place = table_sums.at[dp_peer(k, e)[1]]
+        wires.make(table_first + i, place, place, (dp_peer(k, e)[0], s)).wait_recv()
+    total = table_sums[0]
+    for i in range(1, n.dp):
+        total = total + table_sums[i]
+    table_all[s] = total
+    table_second = wires.reserve(3)
+    for i, (a, b) in enumerate(seq_peers):
+        wires.go(table_second + i, table_all.at[s], table_all.at[s], (d, seq_peer(a, b)))
+    for i, (a, b) in enumerate(seq_peers):
+        place = sums.at[seq_peer(a, b)]
+        wires.make(sums_first + i, place, place, (d, seq_peer(a, b))).wait_recv()
+    mod_total = sums[0]
+    for i in range(1, n.seq):
+        mod_total = mod_total + sums[i]
+    mod_totals = r.mod_totals
+    mod_totals[d] = mod_total
+    totals_first = wires.reserve(len(dp_peers))
+    for i, (k, e) in enumerate(dp_peers):
+        wires.go(totals_first + i, mod_totals.at[d], mod_totals.at[d], (dp_peer(k, e)[0], s))
+    qkv_reduce.finish()
+    for i, (k, e) in enumerate(dp_peers):
+        place = mod_totals.at[dp_peer(k, e)[1]]
+        wires.make(totals_first + i, place, place, (dp_peer(k, e)[0], s)).wait_recv()
+    squashed_rows = r.squashed[pl.ds(pl.multiple_of(d * n.ada_rows, n.ada_rows), n.ada_rows), :]
+    ada = squashed_rows[:, 0:1] * mod_totals[0]
+    for i in range(1, n.dp):
+        ada = ada + squashed_rows[:, i : i + 1] * mod_totals[i]
+    r.grad_ada[...] = ada
+    for i, (a, b) in enumerate(seq_peers):
+        place = table_all.at[seq_peer(a, b)]
+        wires.make(table_second + i, place, place, (d, seq_peer(a, b))).wait_recv()
+    r.table[...] = table_all[...]
+    for reduce in (gate_up_reduce, down_reduce, out_reduce, qkv_reduce):
+        reduce.hand_on()
+    for reduce in (gate_up_reduce, down_reduce, out_reduce, qkv_reduce):
+        reduce.wait()
+    wires.finish()
+
+
+def fused_layer(sizes, valid_len, chain_break, hidden, out_grad, condition, qkv, out, gate_up, down, ada, lines):
+    n = sizes
+    rows, width, length, heads, part, hid = n.rows, n.width, n.length, n.heads, n.part, n.hidden
+    any_space, vmem, smem = pl.ANY, pltpu.VMEM, pltpu.SMEM
+    inputs = dict(
+        valid_len=(valid_len, smem),
+        chain_break=(chain_break, smem),
+        hidden=(hidden, any_space),
+        out_grad=(out_grad, any_space),
+        condition=(condition, any_space),
+        qkv=(qkv, any_space),
+        out=(out, any_space),
+        gate_up=(gate_up, any_space),
+        down=(down, any_space),
+        ada=(ada, vmem),
+        lines=(lines, vmem),
+    )
+    modulations = 6 * width
+
+    def reduced(height, columns):
+        return (
+            ((2, n.far, height, columns), BF16),
+            ((n.far, height, columns), BF16),
+            ((n.far - 1, height, columns), BF16),
+            ((height, columns), BF16),
+        )
+
+    def shares(height, columns):
+        return (n.seq, height, columns), BF16, any_space
+
+    sums = ((2, rows, width), BF16), ((2, rows, width), BF16), ((rows, width), BF16), ((rows, width), BF16)
+    gate_up_sizes, down_sizes = (n.shard, 2 * hid), (n.strip, width)
+    proj_sizes, qkv_sizes = (n.half, width // 2), (n.shard, 3 * part)
+    outputs = dict(
+        result=((rows, width), BF16, vmem),
+        input_grad=((rows, width), BF16, vmem),
+        grad_ada=((n.ada_rows, modulations), F32, vmem),
+        table=((n.seq, heads, 1, LANES), F32, vmem),
+        gate_up_share=shares(*gate_up_sizes),
+        down_share=shares(*down_sizes),
+        proj_share=shares(*proj_sizes),
+        qkv_share=shares(*qkv_sizes),
+    )
+    scratch = dict(
+        w_qkv=((width, 3 * part), BF16),
+        w_out=((n.dp, 2, n.half, width), BF16),
+        w_gate_up=((width, 2 * hid), BF16),
+        w_down=((hid, width), BF16),
+        hidden_all=((length, width), BF16),
+        grads_all=((length, width), BF16),
+        hidden_own=((rows, width), BF16),
+        upstream=((rows, width), BF16),
+        cond_all=((n.dp, 8, n.conditioning), F32),
+        squashed=((n.conditioning, n.dp), F32),
+        mod_send=((n.dp, 1, modulations), F32),
+        mod_recv=((n.dp, 1, modulations), F32),
+        modulation=((1, modulations), F32),
+        mod_sums=((n.seq, 1, modulations), F32),
+        mod_totals=((n.dp, 1, modulations), F32),
+        bias=((heads, (2 * n.blocks - 1) * LANES, LANES), F32),
+        crossed=((heads, 1, LANES), F32),
+        table_sums=((n.dp, heads, 1, LANES), F32),
+        table_all=((n.seq, heads, 1, LANES), F32),
+        keys=((heads, length, DH), BF16),
+        values=((heads, length, DH), BF16),
+        queries=((heads, length, DH), BF16),
+        keys_t=((heads, n.seq, DH, rows), BF16),
+        values_t=((heads, n.seq, DH, rows), BF16),
+        queries_t=((heads, n.seq, DH, rows), BF16),
+        exps=((heads, n.seq, length, rows), BF16),
+        outs_t=((heads, n.seq, DH, rows), F32),
+        inverse=((heads, n.seq, 1, rows), F32),
+        mixed_send=((n.seq, rows, part), BF16),
+        mixed_recv=((n.seq, rows, part), BF16),
+        back_recv=((n.seq, rows, part), BF16),
+        branch=((rows, width), F32),
+        middle=((rows, width), F32),
+        feed_own=((rows, width), F32),
+        second_own=((rows, width), F32),
+        branch_grad=((rows, width), BF16),
+        second_all=((length, width), BF16),
+        second_t=((width, length), BF16),
+        inner=((rows, hid), BF16),
+        inner_t=((hid, length), BF16),
+        gate_up_grads=((length, 2 * hid), BF16),
+        out_near=((n.dp * n.half, width), BF16),
+        out_far=((n.dp * n.half, width // 2), BF16),
+        raw=((length, rows), F32),
+        score_grad=((length, rows), BF16),
+        dots=((heads, rows, DH), BF16),
+        dots_t=((heads, DH, rows), BF16),
+        delta=((heads, 1, rows), F32),
+        pair_grads=((heads, length, 2 * DH), F32),
+        query_grads=((heads, length, DH), BF16),
+        feed_sib=sums[0],
+        feed_got=sums[1],
+        feed_over=sums[2],
+        feed_come=sums[3],
+        second_sib=sums[0],
+        second_got=sums[1],
+        second_over=sums[2],
+        second_come=sums[3],
+        gate_up_grad=reduced(*gate_up_sizes)[0],
+        gate_up_got=reduced(*gate_up_sizes)[1],
+        gate_up_come=reduced(*gate_up_sizes)[2],
+        gate_up_mine=reduced(*gate_up_sizes)[3],
+        down_grad=reduced(*down_sizes)[0],
+        down_got=reduced(*down_sizes)[1],
+        down_come=reduced(*down_sizes)[2],
+        down_mine=reduced(*down_sizes)[3],
+        proj_grad=reduced(*proj_sizes)[0],
+        proj_got=reduced(*proj_sizes)[1],
+        proj_come=reduced(*proj_sizes)[2],
+        proj_mine=reduced(*proj_sizes)[3],
+        qkv_grad=reduced(*qkv_sizes)[0],
+        qkv_got=reduced(*qkv_sizes)[1],
+        qkv_come=reduced(*qkv_sizes)[2],
+        qkv_mine=reduced(*qkv_sizes)[3],
+    )
+    semaphores = dict(send_sem=256, recv_sem=256, local_sem=32)
+    names = [*inputs, *outputs, *scratch, *semaphores]
+    return pl.pallas_call(
+        functools.partial(layer_kernel, n, names),
+        out_shape=[jax.ShapeDtypeStruct(shape, kind) for shape, kind, _ in outputs.values()],
+        in_specs=[pl.BlockSpec(memory_space=space) for _, space in inputs.values()],
+        out_specs=[pl.BlockSpec(memory_space=space) for _, _, space in outputs.values()],
+        scratch_shapes=[pltpu.VMEM(shape, kind) for shape, kind in scratch.values()]
+        + [pltpu.SemaphoreType.DMA((count,)) for count in semaphores.values()],
+        compiler_params=pltpu.CompilerParams(
+            collective_id=0, has_side_effects=True, vmem_limit_bytes=VMEM_LIMIT
+        ),
+    )(*[array for array, _ in inputs.values()])
+
+
+def fused_body(
+    hidden_in,
+    condition,
+    qkv_weight,
+    out_weight,
+    gate_up_weight,
+    down_weight,
+    ada_weight,
+    pair_embed,
+    pair_gain,
+    pair_weight,
+    valid_len,
+    chain_break,
+    out_grad,
+):
+    _, rows, width = hidden_in.shape
+    seq = lax.axis_size("seq")
+    dp = lax.axis_size("dp")
+    me = lax.axis_index("seq")
+    shard = qkv_weight.shape[0]
+    sizes = Sizes(
+        rows, width, seq, dp, shard, down_weight.shape[0], ada_weight.shape[0], condition.shape[1]
+    )
+    heads, part, strip = sizes.heads, sizes.part, sizes.strip
+
+    def pick(array, axis):
+        return lax.dynamic_index_in_dim(array, me, axis, keepdims=False)
+
+    table, pair_pull = jax.vjp(
+        pair_table, pair_embed.astype(F32), pair_gain.astype(F32), pair_weight.astype(F32)
+    )
+    lines = jnp.concatenate(
+        [
+            table[RR : 2 * RR],
+            jnp.zeros((LANES - 2 * RR + 1, H), F32),
+            table[1:RR],
+            table[:1],
+            table[2 * RR :],
+            jnp.zeros((LANES - 3, H), F32),
+        ],
+        axis=0,
+    )
+    lines = lax.dynamic_slice_in_dim(lines.T, me * heads, heads, 0)[:, None, :]
+    y, c = me // 2, lax.rem(me, 2)
+    outs = fused_layer(
+        sizes,
+        valid_len,
+        chain_break,
+        hidden_in[0],
+        out_grad[0],
+        jnp.broadcast_to(condition.astype(F32), (8, condition.shape[1])),
+        pick(qkv_weight.reshape(shard, 3, seq, part), 2).reshape(shard, 3 * part),
+        lax.dynamic_slice(out_weight, (c * sizes.half, y * (width // 2)), (sizes.half, width // 2)),
+        pick(gate_up_weight.reshape(shard, 2, dp, seq, strip), 3).reshape(shard, 2 * sizes.hidden),
+        pick(down_weight.reshape(seq, strip, width), 0),
+        ada_weight,
+        lines,
+    )
+    result, input_grad, grad_ada, table_lines, gate_up_share, down_share, proj_share, qkv_share = outs
+    table_lines = table_lines.reshape(H, LANES)
+    table_grad = jnp.concatenate(
+        [
+            table_lines[:, 40:41],
+            table_lines[:, LANES - RR + 1 :],
+            table_lines[:, :RR],
+            table_lines[:, 41:43],
+        ],
+        axis=1,
+    ).T
+    grad_embed, grad_gain, grad_pair = pair_pull(table_grad)
+    qkv_share = jnp.transpose(qkv_share.reshape(seq, shard, 3, part), (1, 2, 0, 3))
+    proj_share = jnp.transpose(proj_share.reshape(seq // 2, 2, sizes.half, width // 2), (1, 2, 0, 3))
+    gate_up_share = jnp.transpose(gate_up_share.reshape(seq, shard, 2, dp, strip), (1, 2, 3, 0, 4))
+    return (
+        result[None],
+        input_grad[None],
+        qkv_share.reshape(shard, -1).astype(F32),
+        proj_share.reshape(shard, -1).astype(F32),
+        gate_up_share.reshape(shard, -1).astype(F32),
+        down_share.reshape(seq * strip, width).astype(F32),
+        grad_ada,
+        grad_embed,
+        grad_gain,
+        grad_pair,
+    )
+
+
+def body(*arguments):
+    hidden_in, _, qkv_weight, _, _, down_weight = arguments[:6]
+    seq, dp = lax.axis_size("seq"), lax.axis_size("dp")
+    whole_tiles = qkv_weight.shape[0] % 32 == 0 and down_weight.shape[0] % (16 * seq) == 0
+    if whole_tiles and hidden_in.shape[0] == 1 and seq == 4 and dp % 2 == 0:
+        return fused_body(*arguments)
+    return plain_body(*arguments)
+
+
 def solution(mesh):
     rows = P("dp", "seq", None)
     share = P("dp", None)

time: 2050 us -> 229 us (0.11); the launches traced: 2010 us -> 226 us
  local copies, waits for them, and re-layouts: 1330 us -> 31.6 us
  waiting for transfers between devices: 299 us -> 0 us
  blocking collectives: 192 us -> 0 us
  Pallas kernels: 0 us -> 185 us
  matrix products: 103 us -> 2.14 us
  other arithmetic: 66.7 us -> 5.89 us
    unnamed x131 -> x25, local copies, waits for them, and re-layouts: 1100 us -> 3.31 us
    pallas_call x0 -> x1, Pallas kernels: none -> 185 us  [fused_layer(): pl.pallas_call(functools.partial(layer_kernel, n, names), out_shape=[jax....]
    reduce_scatter x7 -> x0, waiting for transfers between devices: 156 us -> none  [scatter(): return lax.psum_scatter(array, name, scatter_dimension=axis, tiled=True)]
    all_gather x9 -> x0, waiting for transfers between devices: 142 us -> none  [the longest x8 142 us: gather(): return lax.all_gather(array, name, axis=axis, tiled=True)]
    all_gather x7 -> x0, blocking collectives: 141 us -> none  [the longest x4 119 us: gather(): return lax.all_gather(array, name, axis=axis, tiled=True)]
    dot_general x20 -> x0, matrix products: 101 us -> none  [the longest x19 100 us: mm(): return jnp.einsum(spec, a, b, preferred_element_type=F32)]
    rev x1 -> x0, local copies, waits for them, and re-layouts: 96 us -> none  [body(): kept[:, :, ::-1]]
    reshape x7 -> x5, local copies, waits for them, and re-layouts: 81.8 us -> 5.98 us  [the longest x1 3.5 us: fused_body(): gate_up_weight.reshape(shard, 2, dp, seq, strip)]
  transfers between devices with their start and end apart: 17 -> 0, of which waited for: 10 -> 0; matrix products, arithmetic and copies ran while one was open for 73% -> 0% of each run, Pallas kernels for 0% -> 0%
where the time goes in v2:
time: 229 us; the launch traced here: 226 us
  Pallas kernels  185 us (81%)
  local copies, waits for them, and re-layouts  31.6 us (14%)
  other arithmetic  5.89 us (3%)
    pallas_call x1, Pallas kernels, fused_layer(): pl.pallas_call(functools.partial(layer_kernel, n, names), out_shape=[jax....  185 us
    convert_element_type x3, local copies, waits for them, and re-layouts, fused_body(): gate_up_share.reshape(shard, -1).astype(F32)  11.7 us

profile of v2, /device:TPU:0, one launch (start us, length us, event | category | flops | bytes accessed | tf_op | source)
XLA Modules:
  0.0 226.4 jit_solution(9302546633179827404)
XLA Ops:
  0.7 1.4 dynamic_slice.19.refs_6_
  2.1 0.9 convert_reduce_fusion
  3.0 1.0 fusion.11
  4.6 1.0 fusion.8
  6.5 3.5 %reshape.91 = bf16[96,2,8,4,96]{4,3,2,1,0:T(4,128)(2,1)S(1)} reshape(bf16[96,6144]{1,0:T(8,128)(2,1)} %param.17) | data formatting | bytes 2359296 | tf_op jit(solution)/shard_map/reshape | solution.py:1297
  10.0 2.6 %dynamic-slice_reduce_fusion = bf16[96,2,8,96]{3,2,1,0:T(8,128)(2,1)S(1)} fusion(bf16[96,2,8,4,96]{4,3,2,1,0:T(4,128)(2,1)S(1)} %reshape.91, s32[]{:T(128)S(6)} %select_n.22), kind=kLoop, calls=%fused_computation | loop fusion | bytes 589828 | tf_op jit(solution)/shard_map/jit(dynamic_index_in_dim)/dynamic_slice | solution.py:1270
  12.6 1.1 reshape.92.refs_7_
  14.9 0.8 copy.36.refs_5_
  15.7 1.6 dynamic-slice_bitcast_fusion.refs_8_
  19.2 184.6 %shard_map.204 = (bf16[256,768]{1,0:T(8,128)(2,1)}, bf16[256,768]{1,0:T(8,128)(2,1)}, f32[32,4608]{1,0:T(8,128)}, f32[4,3,1,128]{3,2,1,0:T(1,128)}, bf16[4,96,15...) custom-call(s32[1]{0:T(128)S(6)} %copy.48.refs_0_, ...), custom_call_target="tpu_custom_call" | custom-call | tf_op jit(solution)/shard_map/pallas_call | solution.py:1231
  203.8 0.7 reduce
  205.2 0.7 fusion.10
  205.9 0.7 broadcast_add_fusion
  206.6 0.8 fusion.6
  207.5 2.7 %reshape.102 = f32[4,96,2,8,96]{4,3,2,1,0:T(8,128)S(1)} reshape(bf16[4,96,1536]{2,1,0:T(8,128)(2,1)} %get-tuple-element.22) | data formatting | bytes 3538944 | tf_op jit(solution)/shard_map/convert_element_type | solution.py:1322
  210.2 3.7 %copy.40 = f32[96,2,8,4,96]{4,3,2,1,0:T(4,128)} copy(f32[96,2,8,4,96]{4,2,1,0,3:T(8,128)S(1)} %bitcast.33) | data formatting | bytes 4718592 | tf_op jit(solution)/shard_map/convert_element_type | solution.py:1322
  213.9 5.2 %reshape.98 = f32[96,6144]{1,0:T(8,128)} reshape(f32[96,2,8,4,96]{4,3,2,1,0:T(4,128)} %copy.40) | data formatting | bytes 4718592 | tf_op jit(solution)/shard_map/convert_element_type | solution.py:1322
  219.4 0.8 copy.38
  220.2 1.7 reshape.96
  221.9 1.1 bitcast_convert_fusion
  223.3 0.7 copy.44
  224.1 0.7 copy.50
  224.8 0.7 copy.51
  225.6 0.8 copy.52
  (47 shorter events, 4.5 us)
Async XLA Ops:
  0.6 4.0 %copy-start = (bf16[256,12]{0,1:T(8,128)(2,1)S(1)}, bf16[256,12]{0,1:T(8,128)(2,1)}, u32[]{:S(2)}) copy-start(bf16[256,12]{0,1:T(8,128)(2,1)} %param.22) | copy-start | bytes 18436
  10.0 3.7 %copy-start.5 = (bf16[96,2304]{1,0:T(8,128)(2,1)S(1)}, bf16[96,2304]{1,0:T(8,128)(2,1)}, u32[]{:S(2)}) copy-start(bf16[96,2304]{1,0:T(8,128)(2,1)} %param.15) | copy-start | bytes 1327108
  13.8 3.5 %copy-start.9 = (bf16[1,256]{1,0:T(2,128)(2,1)S(1)}, bf16[1,256]{1,0:T(2,128)(2,1)}, u32[]{:S(2)}) copy-start(bf16[1,256]{1,0:T(2,128)(2,1)} %param.14) | copy-start | bytes 1540
  14.9 190.0 %copy-start.1 = (bf16[66,256]{1,0:T(8,128)(2,1)S(1)}, bf16[66,256]{1,0:T(8,128)(2,1)}, u32[]{:S(2)}) copy-start(bf16[66,256]{1,0:T(8,128)(2,1)} %param.20) | copy-start | bytes 101380
  213.9 5.2 %copy-start.4 = (bf16[4,96,576]{2,1,0:T(8,128)(2,1)S(1)}, bf16[4,96,576]{2,1,0:T(8,128)(2,1)}, u32[]{:S(2)}) copy-start(bf16[4,96,576]{2,1,0:T(8,128)(2,1)} %get-tuple-element.20) | copy-start | bytes 1327108
  220.2 1.7 copy-start.2
  221.9 1.1 copy-start.8
  223.1 1.0 copy-start.7
  223.1 1.8 copy-start.6
  223.3 2.2 copy-start.3

commit v3 on v2

--- a/solution.py
+++ b/solution.py
@@ -21,10 +21,10 @@
 VMEM_LIMIT = 65400 * 2**10
 
 
-def layer_norm(values):
+def layer_norm(values, epsilon=1e-06):
     average = jnp.mean(values, axis=-1, keepdims=True)
     centered = values - average
-    inv_std = lax.rsqrt(jnp.mean(centered * centered, axis=-1, keepdims=True) + 1e-06)
+    inv_std = lax.rsqrt(jnp.mean(centered * centered, axis=-1, keepdims=True) + epsilon)
     return (centered * inv_std, inv_std)
 
 
@@ -263,6 +263,13 @@
         self.blocks = self.length // LANES
 
 
+def under(where, work):
+    if where is None:
+        work()
+    else:
+        pl.when(where)(work)
+
+
 class Wires:
     def __init__(self, send, recv):
         self.send, self.recv, self.count, self.started = send, recv, 0, []
@@ -282,19 +289,19 @@
             device_id_type=MESH,
         )
 
-    def go(self, number, source, target, device):
+    def go(self, number, source, target, device, where=None):
         copy = self.make(number, source, target, device)
-        copy.start()
-        self.started.append(copy)
+        under(where, copy.start)
+        self.started.append((copy, where))
         return copy
 
     def settle(self, copy):
         copy.wait_send()
-        self.started = [other for other in self.started if other is not copy]
+        self.started = [other for other in self.started if other[0] is not copy]
 
     def finish(self):
-        for copy in self.started:
-            copy.wait_send()
+        for copy, where in self.started:
+            under(where, copy.wait_send)
         self.started = []
 
 
@@ -328,20 +335,45 @@
     def seq_peer(a, b):
         return lax.rem(y + a, 2) * 2 + lax.rem(c + b, 2)
 
+    local_count = [0]
+
+    def local(source, target):
+        copy = pltpu.make_async_copy(source, target, r.local_sem.at[local_count[0]])
+        local_count[0] += 1
+        copy.start()
+        return copy
+
+    qkv_stage, gate_up_stage = r.second_t, r.gate_up_grads
+    staged = [
+        local(r.qkv.at[:, q * width : (q + 1) * width], qkv_stage.at[q * n.shard : (q + 1) * n.shard, 0:width])
+        for q in range(3)
+    ]
+    staged_gate_up = [
+        local(r.gate_up.at[:, q * 2 * hid : (q + 1) * 2 * hid], gate_up_stage.at[q * n.shard : (q + 1) * n.shard])
+        for q in range(n.seq)
+    ]
+    own_shard = pl.ds(pl.multiple_of(d * n.shard, n.shard), n.shard)
+    r.cond_all[d] = jnp.broadcast_to(r.condition[...].astype(F32), (8, n.conditioning))
     barrier = pltpu.get_barrier_semaphore()
     for k, e in dp_peers:
         pl.semaphore_signal(barrier, inc=1, device_id=(dp_peer(k, e)[0], s), device_id_type=MESH)
     for a, b in seq_peers:
         pl.semaphore_signal(barrier, inc=1, device_id=(d, seq_peer(a, b)), device_id_type=MESH)
+    for copy in staged:
+        copy.wait()
+    for side in range(n.seq):
+
+        @pl.when(s == side)
+        def _():
+            r.w_qkv[own_shard, :] = jnp.concatenate(
+                [
+                    qkv_stage[q * n.shard : (q + 1) * n.shard, side * part : (side + 1) * part]
+                    for q in range(3)
+                ],
+                axis=1,
+            )
+
     pl.semaphore_wait(barrier, len(dp_peers) + len(seq_peers))
-
-    local_count = [0]
-
-    def local(source, target):
-        copy = pltpu.make_async_copy(source, target, r.local_sem.at[local_count[0]])
-        local_count[0] += 1
-        copy.start()
-        return copy
 
     class SeqGather:
         def __init__(self, block):
@@ -375,28 +407,95 @@
             self.wait_core()
             self.wait_last()
 
+    last_z = n.far - 1
+
+    class Wave:
+        def __init__(self, block, direct=False):
+            self.block, self.first, self.direct = block, wires.reserve(4), direct
+
+        def send(self, source=None):
+            mine = self.block(z)
+            source = mine if source is None else source
+            wires.go(self.first + 1, source, mine, at_z(1), None if self.direct else z != last_z)
+            wires.go(self.first + 3, source, mine, at_z(3), None if self.direct else z != 0)
+            wires.go(self.first + 2, source, mine, at_z(2))
+
+        def relay(self):
+            place = self.block(z_plus(2))
+            wires.make(self.first + 2, place, place, at_z(2)).wait_recv()
+            if not self.direct:
+                wires.go(self.first, place, place, at_z(1), z == last_z - 1)
+                wires.go(self.first, place, place, at_z(3), z == 1)
+
+        def arrive(self, k):
+            place = self.block(z_plus(n.far - k))
+            far_end = z == (0 if k == 1 else last_z)
+            near = wires.make(self.first + k, place, place, at_z(k))
+            if self.direct:
+                near.wait_recv()
+                return
+            far = wires.make(self.first, place, place, at_z(k))
+            under(far_end, far.wait_recv)
+            under(jnp.logical_not(far_end), near.wait_recv)
+
     class DpGather:
-        def __init__(self, source, place):
-            self.source, self.place, self.first = source, place, wires.reserve(2 * n.far - 1)
+        def __init__(self, source, place, direct=False):
+            self.source, self.place, self.first = source, place, wires.reserve(n.far)
+            self.wave = Wave(lambda zz: place(zz * 2 + x), direct)
 
         def start(self):
             mine = self.place(d)
-            self.own = local(self.source, mine)
-            for k in range(1, n.far):
-                wires.go(self.first + k - 1, self.source, mine, at_z(k))
-            wires.go(self.first + n.far - 1, self.source, mine, at_x)
+            self.own = None if self.source is None else local(self.source, mine)
+            wires.go(self.first, mine if self.source is None else self.source, mine, at_x)
+
+        def along_z(self):
+            self.wave.send(self.source)
+
+        def across(self, k):
+            place = self.place(z_plus(n.far - k) * 2 + x)
+            wires.go(self.first + k, place, place, at_x)
+
+        def relay(self):
+            self.wave.relay()
+            self.across(2)
 
         def hand_on(self):
-            for k in range(1, n.far):
-                place = self.place(dp_peer(k, 0)[1])
-                wires.make(self.first + k - 1, place, place, at_z(k)).wait_recv()
-                wires.go(self.first + n.far - 1 + k, place, place, at_x)
+            for k in (1, 3):
+                self.wave.arrive(k)
+                self.across(k)
+
+        def wait(self):
+            if self.own is not None:
+                self.own.wait()
+            for k in range(n.far):
+                place = self.place(z_plus(n.far - k) * 2 + ox)
+                wires.make(self.first + k, place, place, at_x).wait_recv()
+
+    class DpGatherX:
+        def __init__(self, source, place):
+            self.source, self.place, self.first = source, place, wires.reserve()
+            self.waves = Wave(lambda zz: place(zz * 2 + x)), Wave(lambda zz: place(zz * 2 + ox))
+
+        def start(self):
+            self.own = local(self.source, self.place(d))
+            wires.go(self.first, self.source, self.place(d), at_x)
+
+        def along_z(self):
+            self.waves[0].send(self.source)
+
+        def cross(self):
+            place = self.place(z * 2 + ox)
+            wires.make(self.first, place, place, at_x).wait_recv()
+            self.waves[1].send()
+
+        def relay(self, which):
+            self.waves[which].relay()
 
         def wait(self):
             self.own.wait()
-            for k in range(n.far):
-                place = self.place(dp_peer(k, 1)[1])
-                wires.make(self.first + n.far - 1 + k, place, place, at_x).wait_recv()
+            for wave in self.waves:
+                wave.arrive(1)
+                wave.arrive(3)
 
     class SeqReduce:
         def __init__(self, sib, got, over, come):
@@ -470,7 +569,7 @@
             self.gather.wait_last()
             self.own.wait()
 
-    step = 32
+    step = 64
 
     def by_rows(count, work, start=0, unroll=2):
         def one(q, carry):
@@ -485,7 +584,7 @@
             work(pl.ds(pl.multiple_of(q * wide, wide), wide))
             return 0
 
-        lax.fori_loop(0, count // wide, one, 0)
+        lax.fori_loop(0, count // wide, one, 0, unroll=True)
 
     def fold_rows(array):
         return jnp.sum(array.reshape(step // 8, 8, width), axis=0)
@@ -496,44 +595,56 @@
         return lambda t: ref.at[pl.ds(pl.multiple_of(t * rows, rows), rows)]
 
     hidden_gather, up_gather = SeqGather(rows_of(hidden_all)), SeqGather(rows_of(grads_all))
-    qkv_gather = DpGather(
-        r.qkv, lambda t: r.w_qkv.at[pl.ds(pl.multiple_of(t * n.shard, n.shard), n.shard)]
-    )
+    def shard_rows(ref, height, lanes=slice(None)):
+        return lambda t: ref.at[pl.ds(pl.multiple_of(t * height, height), height), lanes]
+
+    def lane_half(side):
+        return pl.ds(pl.multiple_of(side * (width // 2), width // 2), width // 2)
+
+    lanes_y = lane_half(y)
+    qkv_gathers = [
+        DpGather(None, shard_rows(r.w_qkv, n.shard, lanes), True)
+        for lanes in (slice(0, 2 * LANES), slice(2 * LANES, 3 * part))
+    ]
+    out_gather = DpGather(
+        r.out.at[pl.ds(pl.multiple_of(c * n.half, n.half), n.half), lanes_y],
+        lambda t: r.w_out.at[t, c, :, lanes_y],
+    )
+    half_strip = n.strip // 2
+
+    def down_half(kind, side):
+        low = side * half_strip
+        return kind(
+            r.down.at[pl.ds(pl.multiple_of(s * n.strip + low, half_strip), half_strip)],
+            lambda t: r.w_down.at[pl.ds(pl.multiple_of(t * n.strip + low, half_strip), half_strip)],
+        )
+
+    down_near, down_gather = down_half(DpGather, 0), down_half(DpGatherX, 1)
     pieces = [
-        DpGather(
-            r.gate_up.at[:, pl.ds(q * (hid // 2), hid // 2)],
-            lambda t, q=q: r.w_gate_up.at[
-                pl.ds(pl.multiple_of(t * n.shard, n.shard), n.shard), pl.ds(q * (hid // 2), hid // 2)
-            ],
-        )
-        for q in range(4)
+        DpGather(None, shard_rows(r.w_gate_up, n.shard, slice(q * (hid // 2), (q + 1) * (hid // 2))))
+        for q in (0, 2, 1, 3)
     ]
-    pieces.append(
-        DpGather(r.down, lambda t: r.w_down.at[pl.ds(pl.multiple_of(t * n.strip, n.strip), n.strip)])
-    )
-    lanes_y = pl.ds(pl.multiple_of(y * (width // 2), width // 2), width // 2)
-    out_gather = DpGather(r.out, lambda t: r.w_out.at[t, c, :, lanes_y])
-    pieces.insert(2, out_gather)
 
     def out_block(t):
         ty, tc = t // 2, lax.rem(t, 2)
-        return r.w_out.at[:, tc, :, pl.ds(pl.multiple_of(ty * (width // 2), width // 2), width // 2)]
+        return r.w_out.at[:, tc, :, lane_half(ty)]
 
     out_share = SeqGather(out_block)
 
     cond_first, mod_first = wires.reserve(len(dp_peers)), wires.reserve(len(dp_peers))
     cond_all, mod_send, mod_recv = r.cond_all, r.mod_send, r.mod_recv
-    own_cond = local(r.condition, cond_all.at[d])
     for i, (k, e) in enumerate(dp_peers):
-        wires.go(cond_first + i, r.condition, cond_all.at[d], (dp_peer(k, e)[0], s))
+        wires.go(cond_first + i, cond_all.at[d], cond_all.at[d], (dp_peer(k, e)[0], s))
+    for piece in qkv_gathers:
+        piece.along_z()
+        piece.start()
     own_hidden = local(r.hidden, hidden_gather.block(s))
     keep_hidden = local(r.hidden, r.hidden_own)
     keep_grads = local(r.out_grad, r.upstream)
     hidden_gather.start(r.hidden)
-    qkv_gather.start()
     own_grads = local(r.out_grad, up_gather.block(s))
 
-    own_cond.wait()
+
     for i, (k, e) in enumerate(dp_peers):
         place = cond_all.at[dp_peer(k, e)[1]]
         wires.make(cond_first + i, place, place, (dp_peer(k, e)[0], s)).wait_recv()
@@ -550,22 +661,60 @@
     mod_recv[d] = mod_send[d]
     for i, (k, e) in enumerate(dp_peers):
         wires.go(mod_first + i, mod_send.at[dp_peer(k, e)[0]], mod_recv.at[d], (dp_peer(k, e)[0], s))
-    pieces[0].start()
+    for copy in staged_gate_up:
+        copy.wait()
+    group = n.seq * n.strip
+    for side in range(n.seq):
+
+        @pl.when(s == side)
+        def _():
+            strips = []
+            for number in range(2 * n.dp):
+                block, low = divmod(number * group, 2 * hid)
+                low += side * n.strip
+                strips.append(gate_up_stage[block * n.shard : (block + 1) * n.shard, low : low + n.strip])
+            r.w_gate_up[own_shard, :] = jnp.concatenate(strips, axis=1)
+
+    for piece in (out_gather, *pieces[:2]):
+        piece.start()
+        piece.along_z()
+    down_gather.start()
+    down_gather.along_z()
+    down_near.start()
+    down_near.along_z()
+    for piece in pieces[2:]:
+        piece.start()
     hidden_gather.hand_on()
     up_gather.start(r.out_grad)
-    qkv_gather.hand_on()
-    pieces[1].start()
-
-    bias, lines = r.bias, r.lines
+    for piece in qkv_gathers:
+        piece.relay()
+        piece.hand_on()
+
+    bias, table_t = r.bias, r.table_t
+    embed = r.pair_embed[...].astype(F32)
+    normal, _ = layer_norm(embed, 1e-05)
+    scaled = normal * r.pair_gain[...].astype(F32)
+    scaled = jnp.concatenate([scaled, jnp.zeros((LANES - CLASSES, scaled.shape[1]), F32)], axis=0)
+    table_t[...] = lax.dot_general(
+        r.pair_weight[...].astype(F32),
+        scaled,
+        (((1,), (1,)), ((), ())),
+        precision=HIGHEST,
+        preferred_element_type=F32,
+    )
+
+    def table_line(h):
+        return table_t[pl.ds(s * heads + h, 1), :]
+
     key_in = lax.broadcasted_iota(jnp.int32, (LANES, LANES), 0)
     query_in = lax.broadcasted_iota(jnp.int32, (LANES, LANES), 1)
     middle_tile = n.blocks - 1
 
     def build_bias(h, _):
-        line = lines[h]
-        near = skew(jnp.broadcast_to(line[:, :LANES], (LANES, LANES)), False)
-        low_end = jnp.broadcast_to(line[:, LANES : LANES + 1], (LANES, LANES))
-        high_end = jnp.broadcast_to(line[:, LANES + 1 : LANES + 2], (LANES, LANES))
+        line = table_line(h)
+        near = skew(jnp.broadcast_to(pltpu.roll(line, LANES - RR, 1), (LANES, LANES)), False)
+        low_end = jnp.broadcast_to(line[:, 0:1], (LANES, LANES))
+        high_end = jnp.broadcast_to(line[:, 2 * RR : 2 * RR + 1], (LANES, LANES))
         for tile in range(2 * n.blocks - 1):
             away = tile - middle_tile
             apart = query_in - key_in - away * LANES
@@ -604,8 +753,12 @@
         return 0
 
     by_rows(length, make_first)
-
-    qkv_gather.wait()
+    out_gather.relay()
+    out_gather.hand_on()
+    pieces[0].relay()
+
+    for piece in qkv_gathers:
+        piece.wait()
     w_qkv = r.w_qkv
     keys, values, queries = r.keys, r.values, r.queries
     keys_t, values_t, queries_t = r.keys_t, r.values_t, r.queries_t
@@ -638,6 +791,11 @@
         return 0
 
     lax.fori_loop(0, n.seq, project, 0)
+    pieces[0].hand_on()
+    down_gather.cross()
+    for piece in pieces[2:]:
+        piece.along_z()
+    pieces[1].relay()
 
     valid, broken = r.valid_len[0], r.chain_break[0]
     exps, outs_t, inverse = r.exps, r.outs_t, r.inverse
@@ -661,10 +819,10 @@
         def one_head(h, _):
             for q in range(n.seq):
                 place = slice(q * rows, (q + 1) * rows)
-                raw[place, :] = nn(keys[h, place, :], queries_t[h, t])
+                raw[place, 0:rows] = nn(keys[h, place, :], queries_t[h, t])
             for tile in range(tiles):
                 lanes = slice(tile * LANES, (tile + 1) * LANES)
-                far_side = jnp.broadcast_to(lines[h][:, LANES + 2 : LANES + 3], (1, LANES))
+                far_side = jnp.broadcast_to(table_line(h)[:, CLASSES - 1 : CLASSES], (1, LANES))
                 top = jnp.full((8, LANES), -1e30, F32)
                 for place, strip, key_pos, same in tile_parts(t, tile):
                     logits = raw[place, lanes] + jnp.where(same, bias[h, strip, :], far_side)
@@ -689,6 +847,8 @@
     mixed_send, mixed_recv = r.mixed_send, r.mixed_recv
     mixed_sent = []
     to_send = [at_y, (d, oy * 2 + oc), at_c]
+    out_gather.wait()
+    out_share.start()
     for i, t in enumerate(order):
         attend(t)
         block = jnp.concatenate([outs_t[h, t] for h in range(heads)], axis=0).T.astype(BF16)
@@ -697,13 +857,20 @@
             mixed_sent.append(wires.go(mixed_first + i, mixed_send.at[i], mixed_recv.at[s], to_send[i]))
         else:
             mixed_recv[s] = block
-        pieces[i].hand_on()
-        pieces[i + 2].start()
-    up_gather.hand_on()
-
-    out_gather.wait()
-    out_share.start()
-    out_share.wait()
+        if i == 0:
+            pieces[1].hand_on()
+        if i == 1:
+            down_gather.relay(0)
+        if i == 2:
+            down_near.relay()
+            down_near.hand_on()
+        if i == 0:
+            up_gather.hand_on()
+        if i == 1:
+            out_share.hand_on()
+
+    out_share.wait_core()
+    out_share.wait_last()
 
     def w_out(q, lanes=slice(None)):
         shards = part // n.shard
@@ -735,7 +902,6 @@
     by_rows(rows, make_second)
     second_all[pl.ds(pl.multiple_of(s * rows, rows), rows), :] = r.branch_grad[...]
     second_gather.start()
-    pieces[4].hand_on()
 
     own_grads.wait()
     up_gather.wait_core()
@@ -748,47 +914,43 @@
         return 0
 
     by_rows(length, make_feed_grads)
-    pieces[5].hand_on()
-    for piece in pieces:
-        if piece is not out_gather:
-            piece.wait()
-    second_gather.hand_on()
+    down_gather.relay(1)
+    for piece in (pieces[0], pieces[1], down_near, down_gather):
+        piece.wait()
     w_gate_up, w_down = r.w_gate_up, r.w_down
     inner, inner_t, gate_up_grads, second_t = r.inner, r.inner_t, r.gate_up_grads, r.second_t
     feed_places = (r.feed_sib, r.feed_got, r.feed_over, r.feed_come)
     feed_reduce = SeqReduce(*feed_places)
     second_reduce = SeqReduce(r.second_sib, r.second_got, r.second_over, r.second_come)
-
-    def feed_forward(t, put_second, put_feed):
-        place = pl.ds(pl.multiple_of(t * rows, rows), rows)
-        lanes_t = pl.ds(pl.multiple_of(t * rows, rows), rows)
-        block = second_all[place, :]
-        second_t[:, lanes_t] = block.T
-        given = feed_grads[place, :]
-
-        def units(q, _):
-            low = pl.multiple_of(q * wide, wide)
-            gates, ups, inner_grads = raw.at[0:rows], raw.at[rows : 2 * rows], raw.at[2 * rows : 3 * rows]
-            gates[...] = nn(block, w_gate_up[:, pl.ds(low, wide)])
-            ups[...] = nn(block, w_gate_up[:, pl.ds(low + hid, wide)])
-            inner_grads[...] = nt(given, w_down[pl.ds(low, wide), :])
-            for part_of in range(rows // step):
-                few = slice(part_of * step, (part_of + 1) * step)
-                gate, up, inner_grad = gates[few, :], ups[few, :], inner_grads[few, :]
-                sigmoid = 1.0 / (1.0 + jnp.exp(-gate))
-                silu = gate * sigmoid
-                inner[few, pl.ds(low, wide)] = (silu * up).astype(BF16)
-                to = pl.ds(pl.multiple_of(t * rows + part_of * step, step), step)
-                gate_up_grads[to, pl.ds(low, wide)] = (
-                    inner_grad * up * sigmoid * (1.0 + gate * (1.0 - sigmoid))
-                ).astype(BF16)
-                gate_up_grads[to, pl.ds(low + hid, wide)] = (inner_grad * silu).astype(BF16)
-            inner_t[pl.ds(low, wide), lanes_t] = inner[:, pl.ds(low, wide)].T
-            return 0
-
-        lax.fori_loop(0, hid // wide, units, 0)
-        by_lanes(width, lambda lanes: put_second(lanes, nt(gate_up_grads[place, :], w_gate_up[lanes, :])))
-        by_lanes(width, lambda lanes: put_feed(lanes, nn(inner[...], w_down[:, lanes])))
+    half_hid = hid // 2
+
+    def rows_at(t):
+        return pl.ds(pl.multiple_of(t * rows, rows), rows)
+
+    def units(t, side):
+        place, low = rows_at(t), side * half_hid
+        block, given = second_all[place, :], feed_grads[place, :]
+        gates, ups, inner_grads = (raw.at[i * rows : (i + 1) * rows] for i in range(3))
+        gates[...] = nn(block, w_gate_up[:, low : low + half_hid])
+        ups[...] = nn(block, w_gate_up[:, hid + low : hid + low + half_hid])
+        inner_grads[...] = nt(given, w_down[low : low + half_hid, :])
+        for first_row in range(0, rows, step):
+            few = slice(first_row, first_row + step)
+            gate, up, inner_grad = gates[few, :], ups[few, :], inner_grads[few, :]
+            sigmoid = 1.0 / (1.0 + jnp.exp(-gate))
+            silu = gate * sigmoid
+            to = pl.ds(pl.multiple_of(t * rows + first_row, step), step)
+            inner[to, low : low + half_hid] = (silu * up).astype(BF16)
+            gate_up_grads[to, low : low + half_hid] = (
+                inner_grad * up * sigmoid * (1.0 + gate * (1.0 - sigmoid))
+            ).astype(BF16)
+            gate_up_grads[to, hid + low : hid + low + half_hid] = (inner_grad * silu).astype(BF16)
+
+    def second_part(t, put):
+        by_lanes(width, lambda lanes: put(lanes, nt(gate_up_grads[rows_at(t), :], w_gate_up[lanes, :])))
+
+    def feed_part(t, put):
+        by_lanes(width, lambda lanes: put(lanes, nn(inner[rows_at(t), :], w_down[:, lanes])))
 
     def put_in(ref):
         def put(lanes, block):
@@ -796,20 +958,41 @@
 
         return put
 
-    feed_forward(s, put_in(r.second_own), put_in(r.feed_own))
+    units(s, 0)
     second_gather.wait_core()
-    feed_forward(y * 2 + oc, second_reduce.put_core(0), feed_reduce.put_core(0))
+    units(y * 2 + oc, 0)
+    second_gather.hand_on()
+    pieces[2].relay()
+    units(oy * 2 + c, 0)
+    pieces[2].hand_on()
+    pieces[3].relay()
+    second_gather.wait_last()
+    units(oy * 2 + oc, 0)
+    pieces[3].hand_on()
+    pieces[2].wait()
+    pieces[3].wait()
+    far, over, near = oy * 2 + oc, oy * 2 + c, y * 2 + oc
+    units(far, 1)
+    second_part(far, second_reduce.put_core(1))
+    second_reduce.to_core(1)
+    units(over, 1)
+    second_reduce.wait_far()
+    second_part(over, second_reduce.put_y())
+    second_reduce.to_y()
+    units(near, 1)
+    second_part(near, second_reduce.put_core(0))
     second_reduce.to_core(0)
-    feed_reduce.to_core(0)
-    second_gather.wait_last()
-    feed_forward(oy * 2 + oc, second_reduce.put_core(1), feed_reduce.put_core(1))
-    second_reduce.to_core(1)
-    feed_reduce.to_core(1)
-    second_reduce.wait_far()
-    feed_reduce.wait_far()
-    feed_forward(oy * 2 + c, second_reduce.put_y(), feed_reduce.put_y())
-    second_reduce.to_y()
-    feed_reduce.to_y()
+    units(s, 1)
+    second_part(s, put_in(r.second_own))
+
+    def turn_rows(source, target):
+        def turn(t, _):
+            target[:, rows_at(t)] = source[rows_at(t), :].T
+            return 0
+
+        lax.fori_loop(0, n.seq, turn, 0)
+
+    turn_rows(second_all, second_t)
 
     gate_up_reduce = DpReduce(r.gate_up_grad, r.gate_up_got, r.gate_up_come, r.gate_up_mine, r.gate_up_share)
     down_reduce = DpReduce(r.down_grad, r.down_got, r.down_come, r.down_mine, r.down_share)
@@ -832,8 +1015,17 @@
 
     weight_grad(second_t, gate_up_grads, gate_up_reduce, 2 * hid, wide)
     gate_up_reduce.start()
+    turn_rows(inner, inner_t)
     weight_grad(inner_t, feed_grads, down_reduce, width, wide)
     down_reduce.start()
+    feed_part(far, feed_reduce.put_core(1))
+    feed_reduce.to_core(1)
+    feed_part(near, feed_reduce.put_core(0))
+    feed_reduce.to_core(0)
+    feed_reduce.wait_far()
+    feed_part(over, feed_reduce.put_y())
+    feed_reduce.to_y()
+    feed_part(s, put_in(r.feed_own))
     lax.fori_loop(0, width // (2 * LANES), turn_weight, 0)
 
     sums = r.mod_sums
@@ -886,19 +1078,9 @@
 
     by_lanes(width, make_out_grad)
 
-    feed_reduce.wait()
-
-    def make_result(place, total):
-        feed = feed_reduce.total(r.feed_own, place)
-        r.result[place, :] = (r.middle[place, :] + vector(gate_two) * feed).astype(BF16)
-        return total + fold_rows(upstream[place, :].astype(F32) * feed)
-
-    put_sum(gate_two, by_rows(rows, make_result, empty))
-
     def out_rows(core):
         return out_parts.at[pl.ds(pl.multiple_of(core * quarter, quarter), quarter)]
 
-    wires.go(out_first, out_rows(oc), r.out_near, at_c)
     lanes_oy = pl.ds(pl.multiple_of(oy * (width // 2), width // 2), width // 2)
 
     def out_cores():
@@ -918,7 +1100,7 @@
     pair_grads, query_grads = r.pair_grads, r.query_grads
     bias[...] = jnp.zeros_like(bias)
     pair_grads[...] = jnp.zeros_like(pair_grads)
-    crossed, score_grad = r.crossed, r.score_grad
+    crossed, score_grad = r.crossed, inner.at[:, 0:rows]
     crossed[...] = jnp.zeros_like(crossed)
 
     def attend_back(t):
@@ -933,7 +1115,7 @@
         def one_head(h, _):
             for q in range(n.seq):
                 some = slice(q * rows, (q + 1) * rows)
-                raw[some, :] = nn(values[h, some, :], dots_t[h])
+                raw[some, 0:rows] = nn(values[h, some, :], dots_t[h])
             for tile in range(tiles):
                 lanes = slice(tile * LANES, (tile + 1) * LANES)
                 across = jnp.zeros((8, LANES), F32)
@@ -957,6 +1139,15 @@
 
     gate_up_reduce.along_z(1)
     attend_back(order[3])
+    feed_reduce.wait()
+
+    def make_result(place, total):
+        feed = feed_reduce.total(r.feed_own, place)
+        r.result[place, :] = (r.middle[place, :] + vector(gate_two) * feed).astype(BF16)
+        return total + fold_rows(upstream[place, :].astype(F32) * feed)
+
+    put_sum(gate_two, by_rows(rows, make_result, empty))
+    wires.go(out_first, out_rows(oc), r.out_near, at_c)
     gate_up_reduce.along_z(2)
     out_cores()
     wires.make(back_first + 2, back_recv.at[order[2]], back_recv.at[order[2]], to_send[2]).wait_recv()
@@ -995,12 +1186,7 @@
     first_reduce.to_y()
     first_part(s, put_in(r.feed_own))
 
-    def turn_first(t, _):
-        place = pl.ds(pl.multiple_of(t * rows, rows), rows)
-        second_t[:, place] = first[place, :].T
-        return 0
-
-    lax.fori_loop(0, n.seq, turn_first, 0)
+    turn_rows(first, second_t)
 
     def qkv_grad(q, _):
         low = pl.multiple_of(q * 2 * n.shard, 2 * n.shard)
@@ -1107,7 +1293,53 @@
     wires.finish()
 
 
-def fused_layer(sizes, valid_len, chain_break, hidden, out_grad, condition, qkv, out, gate_up, down, ada, lines):
+def write_outputs(sizes, inputs, outputs):
+    n = sizes
+    result, input_grad, grad_ada, table, gate_up, down, proj, qkv, pair_embed, pair_gain, pair_weight = inputs
+    o_result, o_input, o_qkv, o_out, o_gate_up, o_down, o_ada, o_embed, o_gain, o_pair = outputs
+    o_result[...] = result[...]
+    o_input[...] = input_grad[...]
+    o_ada[...] = grad_ada[...]
+    everyone = range(n.seq)
+    for kind in range(3):
+        lanes = slice(kind * n.part, (kind + 1) * n.part)
+        o_qkv[:, kind * n.width : (kind + 1) * n.width] = jnp.concatenate(
+            [qkv[q, :, lanes] for q in everyone], axis=1
+        ).astype(F32)
+    group = n.seq * n.strip
+    for number in range(2 * n.dp):
+        lanes = slice(number * n.strip, (number + 1) * n.strip)
+        o_gate_up[:, number * group : (number + 1) * group] = jnp.concatenate(
+            [gate_up[q, :, lanes] for q in everyone], axis=1
+        ).astype(F32)
+    for q in everyone:
+        o_down[q * n.strip : (q + 1) * n.strip, :] = down[q].astype(F32)
+        side, core = divmod(q, 2)
+        lanes = slice(side * (n.width // 2), (side + 1) * (n.width // 2))
+        o_out[core * n.half : (core + 1) * n.half, lanes] = proj[q].astype(F32)
+
+    lines = jnp.concatenate([table[q, h] for q in everyone for h in range(n.heads)], axis=0)
+    lane = lax.broadcasted_iota(jnp.int32, lines.shape, 1)
+    table_t = jnp.where(lane < 2 * RR, pltpu.roll(lines, RR, 1), 0.0)
+    for number, at in ((0, 40), (2 * RR, 41), (CLASSES - 1, 42)):
+        table_t = jnp.where(lane == number, jnp.broadcast_to(lines[:, at : at + 1], lines.shape), table_t)
+    embed = pair_embed[...].astype(F32)
+    embed = jnp.concatenate([embed, jnp.zeros((LANES - CLASSES, embed.shape[1]), F32)], axis=0)
+    gain = pair_gain[...].astype(F32)
+    normal, inverted = layer_norm(embed, 1e-05)
+
+    def exact(a, b):
+        return jnp.dot(a, b, precision=HIGHEST, preferred_element_type=F32)
+
+    o_pair[...] = exact(table_t, normal * gain)
+    scaled_grad = exact(table_t.T, pair_weight[...].astype(F32))
+    o_gain[...] = jnp.sum(scaled_grad * normal, axis=0)
+    o_embed[...] = norm_back(scaled_grad * gain, normal, inverted)[0:CLASSES]
+
+
+def fused_layer(
+    sizes, valid_len, chain_break, hidden, out_grad, condition, qkv, out, gate_up, down, ada, embed, gain, weight
+):
     n = sizes
     rows, width, length, heads, part, hid = n.rows, n.width, n.length, n.heads, n.part, n.hidden
     any_space, vmem, smem = pl.ANY, pltpu.VMEM, pltpu.SMEM
@@ -1116,13 +1348,15 @@
         chain_break=(chain_break, smem),
         hidden=(hidden, any_space),
         out_grad=(out_grad, any_space),
-        condition=(condition, any_space),
+        condition=(condition, vmem),
         qkv=(qkv, any_space),
         out=(out, any_space),
         gate_up=(gate_up, any_space),
         down=(down, any_space),
         ada=(ada, vmem),
-        lines=(lines, vmem),
+        pair_embed=(embed, vmem),
+        pair_gain=(gain, vmem),
+        pair_weight=(weight, vmem),
     )
     modulations = 6 * width
 
@@ -1168,6 +1402,7 @@
         mod_totals=((n.dp, 1, modulations), F32),
         bias=((heads, (2 * n.blocks - 1) * LANES, LANES), F32),
         crossed=((heads, 1, LANES), F32),
+        table_t=((H, LANES), F32),
         table_sums=((n.dp, heads, 1, LANES), F32),
         table_all=((n.seq, heads, 1, LANES), F32),
         keys=((heads, length, DH), BF16),
@@ -1189,13 +1424,12 @@
         branch_grad=((rows, width), BF16),
         second_all=((length, width), BF16),
         second_t=((width, length), BF16),
-        inner=((rows, hid), BF16),
+        inner=((length, hid), BF16),
         inner_t=((hid, length), BF16),
         gate_up_grads=((length, 2 * hid), BF16),
         out_near=((n.dp * n.half, width), BF16),
         out_far=((n.dp * n.half, width // 2), BF16),
-        raw=((length, rows), F32),
-        score_grad=((length, rows), BF16),
+        raw=((length, hid // 2), F32),
         dots=((heads, rows, DH), BF16),
         dots_t=((heads, DH, rows), BF16),
         delta=((heads, 1, rows), F32),
@@ -1226,9 +1460,9 @@
         qkv_come=reduced(*qkv_sizes)[2],
         qkv_mine=reduced(*qkv_sizes)[3],
     )
-    semaphores = dict(send_sem=256, recv_sem=256, local_sem=32)
+    semaphores = dict(send_sem=192, recv_sem=192, local_sem=20)
     names = [*inputs, *outputs, *scratch, *semaphores]
-    return pl.pallas_call(
+    made = pl.pallas_call(
         functools.partial(layer_kernel, n, names),
         out_shape=[jax.ShapeDtypeStruct(shape, kind) for shape, kind, _ in outputs.values()],
         in_specs=[pl.BlockSpec(memory_space=space) for _, space in inputs.values()],
@@ -1239,6 +1473,30 @@
             collective_id=0, has_side_effects=True, vmem_limit_bytes=VMEM_LIMIT
         ),
     )(*[array for array, _ in inputs.values()])
+    gradients = (
+        ((rows, width), BF16),
+        ((rows, width), BF16),
+        ((n.shard, 3 * width), F32),
+        ((n.shard, width), F32),
+        ((n.shard, 2 * n.seq * hid), F32),
+        ((n.seq * n.strip, width), F32),
+        ((n.ada_rows, modulations), F32),
+        (embed.shape, F32),
+        (gain.shape, F32),
+        (weight.shape, F32),
+    )
+    count = len(made) + 3
+
+    def write(*refs):
+        write_outputs(n, refs[:count], refs[count:])
+
+    return pl.pallas_call(
+        write,
+        out_shape=[jax.ShapeDtypeStruct(shape, kind) for shape, kind in gradients],
+        in_specs=[pl.BlockSpec(memory_space=vmem)] * count,
+        out_specs=[pl.BlockSpec(memory_space=vmem)] * len(gradients),
+        compiler_params=pltpu.CompilerParams(vmem_limit_bytes=VMEM_LIMIT),
+    )(*made, embed, gain, weight)
 
 
 def fused_body(
@@ -1259,80 +1517,35 @@
     _, rows, width = hidden_in.shape
     seq = lax.axis_size("seq")
     dp = lax.axis_size("dp")
-    me = lax.axis_index("seq")
     shard = qkv_weight.shape[0]
     sizes = Sizes(
         rows, width, seq, dp, shard, down_weight.shape[0], ada_weight.shape[0], condition.shape[1]
     )
-    heads, part, strip = sizes.heads, sizes.part, sizes.strip
-
-    def pick(array, axis):
-        return lax.dynamic_index_in_dim(array, me, axis, keepdims=False)
-
-    table, pair_pull = jax.vjp(
-        pair_table, pair_embed.astype(F32), pair_gain.astype(F32), pair_weight.astype(F32)
-    )
-    lines = jnp.concatenate(
-        [
-            table[RR : 2 * RR],
-            jnp.zeros((LANES - 2 * RR + 1, H), F32),
-            table[1:RR],
-            table[:1],
-            table[2 * RR :],
-            jnp.zeros((LANES - 3, H), F32),
-        ],
-        axis=0,
-    )
-    lines = lax.dynamic_slice_in_dim(lines.T, me * heads, heads, 0)[:, None, :]
-    y, c = me // 2, lax.rem(me, 2)
     outs = fused_layer(
         sizes,
         valid_len,
         chain_break,
         hidden_in[0],
         out_grad[0],
-        jnp.broadcast_to(condition.astype(F32), (8, condition.shape[1])),
-        pick(qkv_weight.reshape(shard, 3, seq, part), 2).reshape(shard, 3 * part),
-        lax.dynamic_slice(out_weight, (c * sizes.half, y * (width // 2)), (sizes.half, width // 2)),
-        pick(gate_up_weight.reshape(shard, 2, dp, seq, strip), 3).reshape(shard, 2 * sizes.hidden),
-        pick(down_weight.reshape(seq, strip, width), 0),
+        condition,
+        qkv_weight,
+        out_weight,
+        gate_up_weight,
+        down_weight,
         ada_weight,
-        lines,
-    )
-    result, input_grad, grad_ada, table_lines, gate_up_share, down_share, proj_share, qkv_share = outs
-    table_lines = table_lines.reshape(H, LANES)
-    table_grad = jnp.concatenate(
-        [
-            table_lines[:, 40:41],
-            table_lines[:, LANES - RR + 1 :],
-            table_lines[:, :RR],
-            table_lines[:, 41:43],
-        ],
-        axis=1,
-    ).T
-    grad_embed, grad_gain, grad_pair = pair_pull(table_grad)
-    qkv_share = jnp.transpose(qkv_share.reshape(seq, shard, 3, part), (1, 2, 0, 3))
-    proj_share = jnp.transpose(proj_share.reshape(seq // 2, 2, sizes.half, width // 2), (1, 2, 0, 3))
-    gate_up_share = jnp.transpose(gate_up_share.reshape(seq, shard, 2, dp, strip), (1, 2, 3, 0, 4))
-    return (
-        result[None],
-        input_grad[None],
-        qkv_share.reshape(shard, -1).astype(F32),
-        proj_share.reshape(shard, -1).astype(F32),
-        gate_up_share.reshape(shard, -1).astype(F32),
-        down_share.reshape(seq * strip, width).astype(F32),
-        grad_ada,
-        grad_embed,
-        grad_gain,
-        grad_pair,
-    )
+        pair_embed,
+        pair_gain,
+        pair_weight.T,
+    )
+    result, input_grad, *grads, grad_gain, grad_pair = outs
+    return (result[None], input_grad[None], *grads, grad_gain, grad_pair.T)
 
 
 def body(*arguments):
     hidden_in, _, qkv_weight, _, _, down_weight = arguments[:6]
     seq, dp = lax.axis_size("seq"), lax.axis_size("dp")
     whole_tiles = qkv_weight.shape[0] % 32 == 0 and down_weight.shape[0] % (16 * seq) == 0
-    if whole_tiles and hidden_in.shape[0] == 1 and seq == 4 and dp % 2 == 0:
+    if whole_tiles and hidden_in.shape[0] == 1 and seq == 4 and dp == 8:
         return fused_body(*arguments)
     return plain_body(*arguments)
 

time: 229 us -> 170 us (0.74)
  local copies, waits for them, and re-layouts: 31.6 us -> 0 us
  Pallas kernels: 185 us -> 167 us
  other arithmetic: 5.89 us -> 0 us
    pallas_call x1, Pallas kernels: 185 us -> 162 us  [fused_layer(): pl.pallas_call(functools.partial(layer_kernel, n, names), out_shape=[jax....]
    convert_element_type x7 -> x0, local copies, waits for them, and re-layouts: 14.6 us -> none  [the longest x3 11.7 us: fused_body(): gate_up_share.reshape(shard, -1).astype(F32)]
    reshape x5 -> x0, local copies, waits for them, and re-layouts: 5.98 us -> none  [the longest x1 3.5 us: fused_body(): gate_up_weight.reshape(shard, 2, dp, seq, strip)]
    pallas_call x0 -> x1, Pallas kernels: none -> 5.65 us  [fused_layer(): pl.pallas_call(write, out_shape=[jax.ShapeDtypeStruct(shape, kind) for sh...]
    dynamic_slice x4 -> x0, local copies, waits for them, and re-layouts: 4.32 us -> none  [the longest x2 2.91 us: pick(): return lax.dynamic_index_in_dim(array, me, axis, keepdims=False)]
    unnamed x25 -> x0, local copies, waits for them, and re-layouts: 3.31 us -> none
    reduce_sum x3 -> x0, other arithmetic: 2.51 us -> none  [the longest x1 0.95 us: pair_table(): jnp.mean(centered * centered, axis=-1, keepdims=True) + 1e-05]
where the time goes in v3:
time: 170 us; the launch traced here: 169 us
  Pallas kernels  167 us (98%)
  between operations  1.98 us (1%)
    pallas_call x1, Pallas kernels, fused_layer(): pl.pallas_call(functools.partial(layer_kernel, n, names), out_shape=[jax....  162 us
    pallas_call x1, Pallas kernels, fused_layer(): pl.pallas_call(write, out_shape=[jax.ShapeDtypeStruct(shape, kind) for sh...  5.65 us

profile of v3, /device:TPU:0, one launch (start us, length us, event | category | flops | bytes accessed | tf_op | source)
XLA Modules:
  0.0 169.1 jit_solution(4691573020052249191)
XLA Ops:
  1.9 161.5 %shard_map.204 = (bf16[256,768]{1,0:T(8,128)(2,1)}, bf16[256,768]{1,0:T(8,128)(2,1)}, f32[32,4608]{1,0:T(8,128)}, f32[4,3,1,128]{3,2,1,0:T(1,128)}, bf16[4,96,15...) custom-call(s32[1]{0:T(128)S(6)} %copy.23.refs_0_, ...), custom_call_target="tpu_custom_call" | custom-call | tf_op jit(solution)/shard_map/pallas_call | solution.py:1465
  163.5 5.7 %shard_map.205 = (bf16[256,768]{1,0:T(8,128)(2,1)}, bf16[256,768]{1,0:T(8,128)(2,1)}, f32[96,2304]{1,0:T(8,128)}, f32[96,768]{1,0:T(8,128)}, f32[96,6144]{1,0:T(...) custom-call(bf16[256,768]{1,0:T(8,128)(2,1)} %get-tuple-element.28.r, ...), custom_call_target="tpu_custom_call" | custom-call | tf_op jit(solution)/shard_map/pallas_call | solution.py:1493
